TPU v7x, 32 devices: a whole 2x2x4 slice. The times are simulated.
32 devices in a mesh: groups: 2 (over x), blk: 16 (over z, y, core).
Axes of the slice: x: 2, y: 2, z: 4, core: 2. Of those that a mesh axis runs over, the one named last changes fastest.
Arguments:
- queries: bfloat16 [32, 8192], P(('groups', 'blk')), parts along dimension 0, may hold values from -100 to 100
- prefix_key_value: bfloat16 [2, 32768, 1024], P(None, ('groups', 'blk')), parts along dimension 1, may hold values from -7 to 7
- suffix_key_value: bfloat16 [32, 2, 512, 1024], P(('groups', 'blk')), parts along dimension 0, may hold values from -9 to 9
- fresh_key_value: bfloat16 [32, 2, 1024], P(('groups', 'blk')), parts along dimension 0, may hold values from -9 to 9
- lengths: int32 [32], P('groups'), parts along dimension 0, may hold values from 1 to 512, 4096 in all
- home: int32 [32], P('groups'), parts along dimension 0, may hold values from 0 to 15, each once
Outputs:
- attended: bfloat16 [32, 8192], P(('groups', 'blk')), parts along dimension 0
There are 2 independent parts, one for each index of `groups`. A program takes and returns all parts, laid end to end along the dimension named above; each array names one. Nothing has to cross between parts.
Inputs may be any that keep to these rules, and one draw needn't show every extreme that they name: Row r's suffix cache lies in slot home[r]; every slot holds exactly one row. `lengths`: some row has exactly 512 suffix tokens.
All inputs are finite; a program needn't handle non-finite values.
Results may differ from a plain program's by a relative error of at most 0.0049.
Values may be sent and summed in bfloat16 or wider, within the bound.
A program may use at most 128 MiB of HBM per device.

v0:
```python
import jax
import jax.numpy as jnp
from jax import lax
from jax.sharding import PartitionSpec as P

QUERY_HEADS = 64
KEY_VALUE_HEADS = 8
HEAD_WIDTH = 128


def per_device(queries, prefix_key_value, suffix_key_value, fresh_key_value, lengths, home):
    rows_per_block = queries.shape[0]
    blocks = lax.axis_size("blk")
    my_index = lax.axis_index("blk")
    revision_count = rows_per_block * blocks
    query_group = QUERY_HEADS // KEY_VALUE_HEADS
    score_scale = HEAD_WIDTH ** (-0.5)
    prefix_length_count = prefix_key_value.shape[1]
    suffix_length_count = suffix_key_value.shape[2]
    gathered_parts = lax.all_gather(queries, "blk", axis=0, tiled=True)
    grouped_queries = gathered_parts.reshape(
        revision_count, KEY_VALUE_HEADS, query_group, HEAD_WIDTH
    )
    query_head_rows = grouped_queries.transpose(1, 0, 2, 3).reshape(
        KEY_VALUE_HEADS, revision_count * query_group, HEAD_WIDTH
    )
    key_head_rows = (
        prefix_key_value[0]
        .reshape(prefix_length_count, KEY_VALUE_HEADS, HEAD_WIDTH)
        .transpose(1, 0, 2)
    )
    value_head_rows = (
        prefix_key_value[1]
        .reshape(prefix_length_count, KEY_VALUE_HEADS, HEAD_WIDTH)
        .transpose(1, 0, 2)
    )

    def prefix_head(item):
        query_block, keys_block, values_block = item
        scores = (
            jnp.dot(query_block, keys_block.T, preferred_element_type=jnp.float32) * score_scale
        )
        peak = jnp.max(scores, axis=-1)
        exponent = jnp.exp(scores - peak[:, None])
        totals = jnp.sum(exponent, axis=-1)
        accum = jnp.dot(
            exponent.astype(jnp.bfloat16), values_block, preferred_element_type=jnp.float32
        )
        return (peak, totals, accum)

    prefix_score_peak, prefix_weight_sum, prefix_accum_sum = lax.map(
        prefix_head, (query_head_rows, key_head_rows, value_head_rows)
    )
    prefix_score_peak = prefix_score_peak.reshape(
        KEY_VALUE_HEADS, revision_count, query_group
    ).transpose(1, 0, 2)
    prefix_weight_sum = prefix_weight_sum.reshape(
        KEY_VALUE_HEADS, revision_count, query_group
    ).transpose(1, 0, 2)
    prefix_accum_sum = prefix_accum_sum.reshape(
        KEY_VALUE_HEADS, revision_count, query_group, HEAD_WIDTH
    ).transpose(1, 0, 2, 3)
    slot_ids = my_index * rows_per_block + jnp.arange(rows_per_block, dtype=jnp.int32)
    row_ids = jnp.arange(revision_count, dtype=jnp.int32)
    matches = home[None, :] == slot_ids[:, None]
    row_lookup = jnp.sum(jnp.where(matches, row_ids[None, :], 0), axis=1)
    slot_queries = grouped_queries[row_lookup]
    slot_key_rows = suffix_key_value[:, 0].reshape(
        rows_per_block, suffix_length_count, KEY_VALUE_HEADS, HEAD_WIDTH
    )
    slot_value_rows = suffix_key_value[:, 1].reshape(
        rows_per_block, suffix_length_count, KEY_VALUE_HEADS, HEAD_WIDTH
    )
    scores = (
        jnp.einsum(
            "rhgd,rthd->rhgt", slot_queries, slot_key_rows, preferred_element_type=jnp.float32
        )
        * score_scale
    )
    live_mask = (
        jnp.arange(suffix_length_count, dtype=jnp.int32)[None, :] < lengths[row_lookup][:, None]
    )
    scores = jnp.where(live_mask[:, None, None, :], scores, -jnp.inf)
    slot_score_peak = jnp.max(scores, axis=-1)
    exponent = jnp.exp(scores - slot_score_peak[..., None])
    slot_weight_sum = jnp.sum(exponent, axis=-1)
    slot_accum_sum = jnp.einsum(
        "rhgt,rthd->rhgd",
        exponent.astype(jnp.bfloat16),
        slot_value_rows,
        preferred_element_type=jnp.float32,
    )
    suffix_score_peak = (
        jnp.full((revision_count, KEY_VALUE_HEADS, query_group), -jnp.inf, jnp.float32)
        .at[row_lookup]
        .set(slot_score_peak)
    )
    suffix_weight_sum = (
        jnp.zeros((revision_count, KEY_VALUE_HEADS, query_group), jnp.float32)
        .at[row_lookup]
        .set(slot_weight_sum)
    )
    suffix_accum_sum = (
        jnp.zeros((revision_count, KEY_VALUE_HEADS, query_group, HEAD_WIDTH), jnp.float32)
        .at[row_lookup]
        .set(slot_accum_sum)
    )
    local_query_rows = queries.reshape(rows_per_block, KEY_VALUE_HEADS, query_group, HEAD_WIDTH)
    fresh_token_keys = fresh_key_value[:, 0].reshape(rows_per_block, KEY_VALUE_HEADS, HEAD_WIDTH)
    fresh_token_values = (
        fresh_key_value[:, 1]
        .reshape(rows_per_block, KEY_VALUE_HEADS, HEAD_WIDTH)
        .astype(jnp.float32)
    )
    local_score_peak = (
        jnp.einsum(
            "rhgd,rhd->rhg", local_query_rows, fresh_token_keys, preferred_element_type=jnp.float32
        )
        * score_scale
    )
    local_accum_sum = jnp.broadcast_to(
        fresh_token_values[:, :, None, :],
        (rows_per_block, KEY_VALUE_HEADS, query_group, HEAD_WIDTH),
    )
    start_offset = my_index * rows_per_block
    new_peak = lax.dynamic_update_slice_in_dim(
        jnp.full((revision_count, KEY_VALUE_HEADS, query_group), -jnp.inf, jnp.float32),
        local_score_peak,
        start_offset,
        0,
    )
    new_total = lax.dynamic_update_slice_in_dim(
        jnp.zeros((revision_count, KEY_VALUE_HEADS, query_group), jnp.float32),
        jnp.ones_like(local_score_peak),
        start_offset,
        0,
    )
    fresh_token_accum = lax.dynamic_update_slice_in_dim(
        jnp.zeros((revision_count, KEY_VALUE_HEADS, query_group, HEAD_WIDTH), jnp.float32),
        local_accum_sum,
        start_offset,
        0,
    )
    peak = jnp.maximum(prefix_score_peak, jnp.maximum(suffix_score_peak, new_peak))
    pre_fac = jnp.exp(prefix_score_peak - peak)
    suf_fac = jnp.exp(suffix_score_peak - peak)
    new_fac = jnp.exp(new_peak - peak)
    totals = pre_fac * prefix_weight_sum + suf_fac * suffix_weight_sum + new_fac * new_total
    accum = (
        pre_fac[..., None] * prefix_accum_sum
        + suf_fac[..., None] * suffix_accum_sum
        + new_fac[..., None] * fresh_token_accum
    )
    normed_half = (
        (accum / totals[..., None])
        .astype(jnp.bfloat16)
        .reshape(revision_count, QUERY_HEADS * HEAD_WIDTH)
    )
    lse = (peak + jnp.log(totals)).reshape(revision_count, QUERY_HEADS)
    landed = lax.all_to_all(
        normed_half.reshape(blocks, rows_per_block, QUERY_HEADS * HEAD_WIDTH),
        "blk",
        split_axis=0,
        concat_axis=0,
        tiled=True,
    )
    landed_lse = lax.all_to_all(
        lse.reshape(blocks, rows_per_block, QUERY_HEADS),
        "blk",
        split_axis=0,
        concat_axis=0,
        tiled=True,
    )
    highest = jnp.max(landed_lse, axis=0)
    weights = jnp.exp(landed_lse - highest[None])
    landed = landed.astype(jnp.float32).reshape(blocks, rows_per_block, QUERY_HEADS, HEAD_WIDTH)
    numerator = jnp.sum(weights[..., None] * landed, axis=0)
    denominator = jnp.sum(weights, axis=0)
    result = numerator / denominator[..., None]
    return result.reshape(rows_per_block, QUERY_HEADS * HEAD_WIDTH).astype(jnp.bfloat16)


def solution(mesh):
    placed = (
        P(("groups", "blk"), None),
        P(None, ("groups", "blk"), None),
        P(("groups", "blk"), None, None, None),
        P(("groups", "blk"), None, None),
        P("groups"),
        P("groups"),
    )
    return jax.shard_map(
        per_device,
        mesh=mesh,
        in_specs=placed,
        out_specs=P(("groups", "blk"), None),
        check_vma=False,
    )
```

profile of v0, /device:TPU:0, one launch (start us, length us, event | category | flops | bytes accessed | tf_op | source)
XLA Modules:
  0.0 108.4 jit_solution(14778481534086391625)
XLA Ops:
  0.0 1.3 %fusion.34 = s32[]{:T(128)} fusion(s32[16]{0:T(128)} %param.19, s32[]{:T(128)S(6)} %axis_index.12), kind=kLoop, calls=%fused_computation.58 | loop fusion | flops 47 | bytes 72 | tf_op jit(solution)/shard_map/reduce_sum | solution.py:66
  3.2 1.2 %dynamic-slice.24 = s32[1]{0:T(128)} dynamic-slice(s32[16]{0:T(128)} %param.18, s32[]{:T(128)} %bitcast.15), dynamic_slice_sizes={1} | dynamic-slice | bytes 12 | tf_op jit(solution)/shard_map/gather | solution.py:81
  4.5 1.1 %iota_compare_fusion = pred[512]{0:T(512)(128)(4,1)} fusion(s32[]{:T(128)} %bitcast.16), kind=kLoop, calls=%fused_computation.53 | loop fusion | flops 512 | bytes 516 | tf_op jit(solution)/shard_map/lt | solution.py:81
  5.6 1.7 %fusion.40 = (bf16[1,1,512,1024]{3,2,1,0:T(8,128)(2,1)S(1)}, bf16[1,1,512,1024]{3,2,1,0:T(8,128)(2,1)S(1)}) fusion(bf16[1,2,512,1024]{3,2,1,0:T(8,128)(2,1)} %param.16), kind=kLoop, calls=%fused_computation.62 | loop fusion | bytes 4194304 | tf_op jit(solution)/shard_map/slice | solution.py:71
  7.4 0.5 copy.117
  8.1 24.6 %all-gather = bf16[16,1,8192]{2,1,0:T(2,128)(2,1)S(1)} all-gather(bf16[1,1,8192]{2,1,0:T(2,128)(2,1)S(1)} %bitcast.126), channel_id=1, replica_groups=mesh['groups'=2,'blk'=16] {'blk'}, dimensions={0}, use_global_device_ids=true | all-gather | bytes 278528 | tf_op jit(solution)/shard_map/all_gather | solution.py:20
  32.7 1.5 %reduce.26 = bf16[16,8192]{1,0:T(8,128)(2,1)S(1)} reduce(bf16[16,1,8192]{2,1,0:T(2,128)(2,1)S(1)} %all-gather, bf16[]{:T(256)} %constant.147), dimensions={1}, to_apply=%all-gather.reduce_sub_computation | reduce | bytes 524290 | tf_op jit(solution)/shard_map/all_gather | solution.py:20
  34.3 0.7 and_reduce_fusion.1
  35.0 0.9 fusion.41
  36.1 0.7 select_bitcast_fusion
  36.8 0.7 copy.96
  37.5 0.7 copy.99
  38.4 0.7 copy.97
  39.1 4.0 %fusion.39 = (bf16[1,1024,1024]{2,1,0:T(8,128)(2,1)S(1)}, bf16[1,1024,1024]{2,1,0:T(8,128)(2,1)}) fusion(bf16[2,1024,1024]{2,1,0:T(8,128)(2,1)} %param.15), kind=kLoop, calls=%fused_computation.61 | loop fusion | bytes 8388608 | tf_op jit(solution)/shard_map/slice | solution.py:33
  43.0 4.0 %copy.115 = bf16[1,1024,1024]{1,2,0:T(8,128)(2,1)} copy(bf16[1,1024,1024]{2,1,0:T(8,128)(2,1)} %get-tuple-element.164) | data formatting | bytes 4194304
  47.0 2.6 %copy.116 = bf16[1,1024,1024]{1,2,0:T(8,128)(2,1)} copy(bf16[1,1024,1024]{2,1,0:T(8,128)(2,1)S(1)} %get-tuple-element.163) | data formatting | bytes 4194304
  49.7 27.4 %while.19 = (s32[]{:T(128)}, f32[8,128]{1,0:T(8,128)S(1)}, f32[8,128]{1,0:T(8,128)S(1)}, f32[8,128,128]{2,1,0:T(8,128)}, bf16[8,128,128]{2,1,0:T(8,128)(2,1)S(1)...) while((s32[]{:T(128)}, f32[8,128]{1,0:T(8,128)S(1)}, ...), condition=%wide.region_3.4_spmd, body=%wide.region_0.3_spmd.sunk | while | flops 67895040 | bytes 2201701 | solution.py:51
  49.7 1.3 %fusion.52 = (f32[128]{0:T(128)S(1)}, f32[128,1024]{1,0:T(8,128)S(1)}) fusion(bf16[8,1024,128]{1,2,0:T(8,128)(2,1)} %get-tuple-element.241, s32[]{:T(128)} %get-tuple-element.227, bf16[8,128,128]{2,1,0:T(8,128)(2,1)S(1)} %get-tuple-element.240), kind=kOutput, calls=%fused_computation.60.clone.1 | convolution fusion | flops 33816448 | bytes 820736 | tf_op jit(solution)/shard_map/while/body/eval_jaxpr/dot_general | solution.py:41
  50.9 1.9 %fusion.54 = f32[8,128,128]{2,1,0:T(8,128)} fusion(f32[8,128,128]{2,1,0:T(8,128)} %get-tuple-element.230, s32[]{:T(128)} %get-tuple-element.227, f32[128,1024]{1,0:T(8,128)S(1)} %get-tuple-element.217, bf16[8,1024,128]{1,2,0:T(8,128)(2,1)} %get-tuple-element.242, f32[128]{0:T(128)S(1)} %get-tuple-element.216), kind=kOutput, calls=%fused_computation.2.clone.1 | convolution fusion | flops 33816576 | bytes 853504 | tf_op jit(solution)/shard_map/while/body/eval_jaxpr/dot_general | solution.py:46
  53.1 1.2 %fusion.52 = (f32[128]{0:T(128)S(1)}, f32[128,1024]{1,0:T(8,128)S(1)}) fusion(bf16[8,1024,128]{1,2,0:T(8,128)(2,1)} %get-tuple-element.241, s32[]{:T(128)} %get-tuple-element.227, bf16[8,128,128]{2,1,0:T(8,128)(2,1)S(1)} %get-tuple-element.240), kind=kOutput, calls=%fused_computation.60.clone.1 | convolution fusion | flops 33816448 | bytes 820736 | tf_op jit(solution)/shard_map/while/body/eval_jaxpr/dot_general | solution.py:41
  54.4 1.9 %fusion.54 = f32[8,128,128]{2,1,0:T(8,128)} fusion(f32[8,128,128]{2,1,0:T(8,128)} %get-tuple-element.230, s32[]{:T(128)} %get-tuple-element.227, f32[128,1024]{1,0:T(8,128)S(1)} %get-tuple-element.217, bf16[8,1024,128]{1,2,0:T(8,128)(2,1)} %get-tuple-element.242, f32[128]{0:T(128)S(1)} %get-tuple-element.216), kind=kOutput, calls=%fused_computation.2.clone.1 | convolution fusion | flops 33816576 | bytes 853504 | tf_op jit(solution)/shard_map/while/body/eval_jaxpr/dot_general | solution.py:46
  56.6 1.2 %fusion.52 = (f32[128]{0:T(128)S(1)}, f32[128,1024]{1,0:T(8,128)S(1)}) fusion(bf16[8,1024,128]{1,2,0:T(8,128)(2,1)} %get-tuple-element.241, s32[]{:T(128)} %get-tuple-element.227, bf16[8,128,128]{2,1,0:T(8,128)(2,1)S(1)} %get-tuple-element.240), kind=kOutput, calls=%fused_computation.60.clone.1 | convolution fusion | flops 33816448 | bytes 820736 | tf_op jit(solution)/shard_map/while/body/eval_jaxpr/dot_general | solution.py:41
  57.8 1.9 %fusion.54 = f32[8,128,128]{2,1,0:T(8,128)} fusion(f32[8,128,128]{2,1,0:T(8,128)} %get-tuple-element.230, s32[]{:T(128)} %get-tuple-element.227, f32[128,1024]{1,0:T(8,128)S(1)} %get-tuple-element.217, bf16[8,1024,128]{1,2,0:T(8,128)(2,1)} %get-tuple-element.242, f32[128]{0:T(128)S(1)} %get-tuple-element.216), kind=kOutput, calls=%fused_computation.2.clone.1 | convolution fusion | flops 33816576 | bytes 853504 | tf_op jit(solution)/shard_map/while/body/eval_jaxpr/dot_general | solution.py:46
  60.0 1.2 %fusion.52 = (f32[128]{0:T(128)S(1)}, f32[128,1024]{1,0:T(8,128)S(1)}) fusion(bf16[8,1024,128]{1,2,0:T(8,128)(2,1)} %get-tuple-element.241, s32[]{:T(128)} %get-tuple-element.227, bf16[8,128,128]{2,1,0:T(8,128)(2,1)S(1)} %get-tuple-element.240), kind=kOutput, calls=%fused_computation.60.clone.1 | convolution fusion | flops 33816448 | bytes 820736 | tf_op jit(solution)/shard_map/while/body/eval_jaxpr/dot_general | solution.py:41
  61.2 1.9 %fusion.54 = f32[8,128,128]{2,1,0:T(8,128)} fusion(f32[8,128,128]{2,1,0:T(8,128)} %get-tuple-element.230, s32[]{:T(128)} %get-tuple-element.227, f32[128,1024]{1,0:T(8,128)S(1)} %get-tuple-element.217, bf16[8,1024,128]{1,2,0:T(8,128)(2,1)} %get-tuple-element.242, f32[128]{0:T(128)S(1)} %get-tuple-element.216), kind=kOutput, calls=%fused_computation.2.clone.1 | convolution fusion | flops 33816576 | bytes 853504 | tf_op jit(solution)/shard_map/while/body/eval_jaxpr/dot_general | solution.py:46
  63.4 1.2 %fusion.52 = (f32[128]{0:T(128)S(1)}, f32[128,1024]{1,0:T(8,128)S(1)}) fusion(bf16[8,1024,128]{1,2,0:T(8,128)(2,1)} %get-tuple-element.241, s32[]{:T(128)} %get-tuple-element.227, bf16[8,128,128]{2,1,0:T(8,128)(2,1)S(1)} %get-tuple-element.240), kind=kOutput, calls=%fused_computation.60.clone.1 | convolution fusion | flops 33816448 | bytes 820736 | tf_op jit(solution)/shard_map/while/body/eval_jaxpr/dot_general | solution.py:41
  64.7 1.9 %fusion.54 = f32[8,128,128]{2,1,0:T(8,128)} fusion(f32[8,128,128]{2,1,0:T(8,128)} %get-tuple-element.230, s32[]{:T(128)} %get-tuple-element.227, f32[128,1024]{1,0:T(8,128)S(1)} %get-tuple-element.217, bf16[8,1024,128]{1,2,0:T(8,128)(2,1)} %get-tuple-element.242, f32[128]{0:T(128)S(1)} %get-tuple-element.216), kind=kOutput, calls=%fused_computation.2.clone.1 | convolution fusion | flops 33816576 | bytes 853504 | tf_op jit(solution)/shard_map/while/body/eval_jaxpr/dot_general | solution.py:46
  66.8 1.2 %fusion.52 = (f32[128]{0:T(128)S(1)}, f32[128,1024]{1,0:T(8,128)S(1)}) fusion(bf16[8,1024,128]{1,2,0:T(8,128)(2,1)} %get-tuple-element.241, s32[]{:T(128)} %get-tuple-element.227, bf16[8,128,128]{2,1,0:T(8,128)(2,1)S(1)} %get-tuple-element.240), kind=kOutput, calls=%fused_computation.60.clone.1 | convolution fusion | flops 33816448 | bytes 820736 | tf_op jit(solution)/shard_map/while/body/eval_jaxpr/dot_general | solution.py:41
  68.1 1.9 %fusion.54 = f32[8,128,128]{2,1,0:T(8,128)} fusion(f32[8,128,128]{2,1,0:T(8,128)} %get-tuple-element.230, s32[]{:T(128)} %get-tuple-element.227, f32[128,1024]{1,0:T(8,128)S(1)} %get-tuple-element.217, bf16[8,1024,128]{1,2,0:T(8,128)(2,1)} %get-tuple-element.242, f32[128]{0:T(128)S(1)} %get-tuple-element.216), kind=kOutput, calls=%fused_computation.2.clone.1 | convolution fusion | flops 33816576 | bytes 853504 | tf_op jit(solution)/shard_map/while/body/eval_jaxpr/dot_general | solution.py:46
  70.3 1.2 %fusion.52 = (f32[128]{0:T(128)S(1)}, f32[128,1024]{1,0:T(8,128)S(1)}) fusion(bf16[8,1024,128]{1,2,0:T(8,128)(2,1)} %get-tuple-element.241, s32[]{:T(128)} %get-tuple-element.227, bf16[8,128,128]{2,1,0:T(8,128)(2,1)S(1)} %get-tuple-element.240), kind=kOutput, calls=%fused_computation.60.clone.1 | convolution fusion | flops 33816448 | bytes 820736 | tf_op jit(solution)/shard_map/while/body/eval_jaxpr/dot_general | solution.py:41
  71.5 1.9 %fusion.54 = f32[8,128,128]{2,1,0:T(8,128)} fusion(f32[8,128,128]{2,1,0:T(8,128)} %get-tuple-element.230, s32[]{:T(128)} %get-tuple-element.227, f32[128,1024]{1,0:T(8,128)S(1)} %get-tuple-element.217, bf16[8,1024,128]{1,2,0:T(8,128)(2,1)} %get-tuple-element.242, f32[128]{0:T(128)S(1)} %get-tuple-element.216), kind=kOutput, calls=%fused_computation.2.clone.1 | convolution fusion | flops 33816576 | bytes 853504 | tf_op jit(solution)/shard_map/while/body/eval_jaxpr/dot_general | solution.py:46
  73.7 1.2 %fusion.52 = (f32[128]{0:T(128)S(1)}, f32[128,1024]{1,0:T(8,128)S(1)}) fusion(bf16[8,1024,128]{1,2,0:T(8,128)(2,1)} %get-tuple-element.241, s32[]{:T(128)} %get-tuple-element.227, bf16[8,128,128]{2,1,0:T(8,128)(2,1)S(1)} %get-tuple-element.240), kind=kOutput, calls=%fused_computation.60.clone.1 | convolution fusion | flops 33816448 | bytes 820736 | tf_op jit(solution)/shard_map/while/body/eval_jaxpr/dot_general | solution.py:41
  74.9 1.9 %fusion.54 = f32[8,128,128]{2,1,0:T(8,128)} fusion(f32[8,128,128]{2,1,0:T(8,128)} %get-tuple-element.230, s32[]{:T(128)} %get-tuple-element.227, f32[128,1024]{1,0:T(8,128)S(1)} %get-tuple-element.217, bf16[8,1024,128]{1,2,0:T(8,128)(2,1)} %get-tuple-element.242, f32[128]{0:T(128)S(1)} %get-tuple-element.216), kind=kOutput, calls=%fused_computation.2.clone.1 | convolution fusion | flops 33816576 | bytes 853504 | tf_op jit(solution)/shard_map/while/body/eval_jaxpr/dot_general | solution.py:46
  77.5 0.6 scatter.10
  78.1 0.6 scatter.11
  79.0 0.7 copy.100
  79.7 3.5 %all-to-all-start = ((f32[16,1,64]{2,1,0:T(1,128)}), f32[16,1,64]{2,1,0:T(1,128)S(1)}, u32[]{:S(2)}, u32[]{:S(2)}) async-start(f32[16,1,64]{2,1,0:T(1,128)} %copy.100), calls=%async_computation | async-start | bytes 16384 | tf_op jit(solution)/shard_map/all_to_all | solution.py:167
  83.6 0.7 and_reduce_fusion
  84.3 0.5 copy.118
  84.9 1.0 fusion.15
  85.9 0.7 fusion.19
  86.7 0.6 broadcast.203
  87.3 2.2 %reduce.30 = bf16[16,8192]{1,0:T(8,128)(2,1)S(1)} reduce(bf16[16,1,8192]{2,1,0:T(2,128)(2,1)S(1)} %reshape_reshape.8, bf16[]{:T(256)} %broadcast.203), dimensions={1}, to_apply=%reshape_reshape.8.reduce_sub_computation | reduce | bytes 524290 | tf_op jit(solution)/shard_map/reshape;reshape | solution.py:161
  89.5 0.9 reshape.327
  90.4 6.0 %all-to-all-start.1 = ((bf16[16,2,4096]{2,1,0:T(2,128)(2,1)}), bf16[16,2,4096]{2,1,0:T(2,128)(2,1)S(1)}, u32[]{:S(2)}, u32[]{:S(2)}) async-start(bf16[16,2,4096]{2,1,0:T(2,128)(2,1)} %reshape.327), calls=%async_computation.1 | async-start | bytes 524288 | tf_op jit(solution)/shard_map/all_to_all | solution.py:160
  96.4 10.0 %all-to-all-done.1 = bf16[16,2,4096]{2,1,0:T(2,128)(2,1)S(1)} async-done(((bf16[16,2,4096]{2,1,0:T(2,128)(2,1)}), bf16[16,2,4096]{2,1,0:T(2,128)(2,1)S(1)}, u32[]{:S(2)}, u32[]{:S(2)}) %all-to-all-start.1) | async-done | bytes 262176 | tf_op jit(solution)/shard_map/all_to_all | solution.py:160
  106.9 0.8 multiply_reduce_fusion
  107.8 0.7 divide_convert_fusion
  (76 shorter events, 4.8 us)
Async XLA Ops:
  7.3 0.8 copy-start.1
  7.3 27.0 %copy-start.7 = (s32[3]{0:T(128)S(1)}, s32[3]{0:T(128)}, u32[]{:S(2)}) copy-start(s32[3]{0:T(128)} %constant.101.clone.1) | copy-start | bytes 40
  7.9 30.3 %copy-start.5 = (bf16[1,2,1024]{2,1,0:T(2,128)(2,1)S(1)}, bf16[1,2,1024]{2,1,0:T(2,128)(2,1)}, u32[]{:S(2)}) copy-start(bf16[1,2,1024]{2,1,0:T(2,128)(2,1)} %param.17) | copy-start | bytes 12292
  49.6 27.8 %copy-start.4 = (f32[1,8,8]{0,2,1:T(8,128)S(1)}, f32[1,8,8]{0,2,1:T(8,128)}, u32[]{:S(2)}) copy-start(f32[1,8,8]{0,2,1:T(8,128)} %copy.96) | copy-start | bytes 772
  49.6 28.4 %copy-start.2 = (f32[1,8,8]{0,2,1:T(8,128)S(1)}, f32[1,8,8]{0,2,1:T(8,128)}, u32[]{:S(2)}) copy-start(f32[1,8,8]{0,2,1:T(8,128)} %copy.99) | copy-start | bytes 772
  49.7 29.1 %copy-start.3 = (f32[1,8,8]{0,2,1:T(8,128)S(1)}, f32[1,8,8]{0,2,1:T(8,128)}, u32[]{:S(2)}) copy-start(f32[1,8,8]{0,2,1:T(8,128)} %copy.97) | copy-start | bytes 772
  49.7 33.9 %copy-start.6 = (s32[4]{0:T(128)S(1)}, s32[4]{0:T(128)}, u32[]{:S(2)}) copy-start(s32[4]{0:T(128)} %constant.106.clone.1) | copy-start | bytes 52
  79.7 10.7 %all-to-all-start = ((f32[16,1,64]{2,1,0:T(1,128)}), f32[16,1,64]{2,1,0:T(1,128)S(1)}, u32[]{:S(2)}, u32[]{:S(2)}) async-start(f32[16,1,64]{2,1,0:T(1,128)} %copy.100), calls=%async_computation | async-start | bytes 16384 | tf_op jit(solution)/shard_map/all_to_all | solution.py:167
  84.3 1.6 %copy-start = (f32[8,128,128]{2,1,0:T(8,128)S(1)}, f32[8,128,128]{2,1,0:T(8,128)}, u32[]{:S(2)}) copy-start(f32[8,128,128]{2,1,0:T(8,128)} %get-tuple-element.82) | copy-start | bytes 1572868
  90.4 16.0 %all-to-all-start.1 = ((bf16[16,2,4096]{2,1,0:T(2,128)(2,1)}), bf16[16,2,4096]{2,1,0:T(2,128)(2,1)S(1)}, u32[]{:S(2)}, u32[]{:S(2)}) async-start(bf16[16,2,4096]{2,1,0:T(2,128)(2,1)} %reshape.327), calls=%async_computation.1 | async-start | bytes 524288 | tf_op jit(solution)/shard_map/all_to_all | solution.py:160
where the time goes:
time: 109 us; the launch traced here: 108 us
  matrix products  26.9 us (25%)
  blocking collectives  24.6 us (23%)
  local copies, waits for them, and re-layouts  22.6 us (21%)
  other arithmetic  12.5 us (11%)
  waiting for transfers between devices  9.97 us (9%)
  starting transfers between devices  9.44 us (9%)
  between operations  2.32 us (2%)
    all_gather x1, blocking collectives, per_device(): gathered_parts = lax.all_gather(queries, 'blk', axis=0, tiled=True)  24.6 us
    dot_general x8, matrix products, prefix_head(): jnp.dot(exponent.astype(jnp.bfloat16), values_block, preferred_element_ty...  14.9 us
    dot_general x8, matrix products, prefix_head(): jnp.dot(query_block, keys_block.T, preferred_element_type=jnp.float32)  9.99 us
    all_to_all x1, waiting for transfers between devices, per_device(): lax.all_to_all(normed_half.reshape(blocks, rows_per_block, QUERY_HEADS *...  9.97 us
    unnamed x23, local copies, waits for them, and re-layouts  9.02 us
    all_to_all x1, starting transfers between devices, per_device(): lax.all_to_all(normed_half.reshape(blocks, rows_per_block, QUERY_HEADS *...  5.97 us
    slice x1, local copies, waits for them, and re-layouts, per_device(): prefix_key_value[1]  3.96 us
    all_to_all x1, starting transfers between devices, per_device(): lax.all_to_all(lse.reshape(blocks, rows_per_block, QUERY_HEADS), 'blk', s...  3.47 us
  transfers between devices with their start and end apart: 2, of which 1 were waited for; matrix products, arithmetic and copies ran while one was open for 7% of the time, Pallas kernels for 0%

commit v1 on v0

v1 whole, which is shorter than its diff:
```python
import functools

import jax
import jax.numpy as jnp
from jax import lax
from jax.experimental import pallas as pl
from jax.experimental.pallas import tpu as pltpu
from jax.sharding import PartitionSpec as P

QUERY_HEADS = 64
KEY_VALUE_HEADS = 8
HEAD_WIDTH = 128
GROUP = QUERY_HEADS // KEY_VALUE_HEADS
SCALE = HEAD_WIDTH ** (-0.5)
LOG2E = 1.4426950408889634
TILE = 2 * GROUP
PAIRS = KEY_VALUE_HEADS // 2
LSE_ROWS = 16
QUERY_CHUNKS = 4
OUT_CHUNKS = 4


def kernel(n, home_ref, lengths_ref, q_ref, fresh_ref, prefix_ref, suffix_ref, out_ref,
           obuf, rbuf, lbuf, kbuf, vbuf, skbuf, svbuf,
           load_sem, qsend, qrecv, osend, orecv, *qbufs):
    me = lax.axis_index("blk")
    f32, bf16 = jnp.float32, jnp.bfloat16
    loads = [
        pltpu.make_async_copy(prefix_ref.at[0], kbuf, load_sem.at[0]),
        pltpu.make_async_copy(prefix_ref.at[1], vbuf, load_sem.at[1]),
        pltpu.make_async_copy(suffix_ref.at[0, 0], skbuf, load_sem.at[2]),
        pltpu.make_async_copy(suffix_ref.at[0, 1], svbuf, load_sem.at[3]),
    ]
    for load in loads:
        load.start()

    barrier = pltpu.get_barrier_semaphore()

    def greet(k, _):
        peer = lax.rem(me + k, n)
        pl.semaphore_signal(barrier, inc=1, device_id={"blk": peer},
                            device_id_type=pl.DeviceIdType.MESH)
        return 0

    lax.fori_loop(1, n, greet, 0)

    def find(r, carry):
        row, length = carry
        here = home_ref[r] == me
        return jnp.where(here, r, row), jnp.where(here, lengths_ref[r], length)

    slot_row, slot_len = lax.fori_loop(0, n, find, (jnp.int32(0), jnp.int32(0)))

    pl.semaphore_wait(barrier, n - 1)

    q_rows = QUERY_HEADS // QUERY_CHUNKS

    def q_send(c):
        rows = pl.ds(c * q_rows, q_rows)

        def body(k, _):
            peer = lax.rem(me + k, n)
            pltpu.make_async_remote_copy(
                src_ref=q_ref.at[rows], dst_ref=qbufs[c].at[me],
                send_sem=qsend.at[c], recv_sem=qrecv.at[c],
                device_id={"blk": peer}, device_id_type=pl.DeviceIdType.MESH,
            ).start()
            return 0

        lax.fori_loop(1, n, body, 0)

    for c in range(QUERY_CHUNKS):
        q_send(c)
        qbufs[c][me] = q_ref[pl.ds(c * q_rows, q_rows), :]

    def q_wait(sem, c):
        part = qbufs[c].at[pl.ds(0, n - 1)]
        pltpu.make_async_copy(part, part, sem.at[c]).wait()

    o_rows = QUERY_HEADS // OUT_CHUNKS

    def o_span(c):
        extra = LSE_ROWS if c == OUT_CHUNKS - 1 else 0
        return pl.ds(c * o_rows, o_rows + extra)

    def o_send(c):
        rows = o_span(c)

        def body(k, _):
            peer = lax.rem(me + k, n)
            pltpu.make_async_remote_copy(
                src_ref=obuf.at[peer, rows], dst_ref=rbuf.at[me, rows],
                send_sem=osend.at[c], recv_sem=orecv.at[c],
                device_id={"blk": peer}, device_id_type=pl.DeviceIdType.MESH,
            ).start()
            return 0

        lax.fori_loop(1, n, body, 0)

    def o_wait(sem, c):
        part = rbuf.at[pl.ds(0, n - 1), o_span(c)]
        pltpu.make_async_copy(part, part, sem.at[c]).wait()

    batch = 16 if n % 16 == 0 else n
    live = lax.broadcasted_iota(jnp.int32, (GROUP, skbuf.shape[0]), 1) < slot_len
    lane = lax.broadcasted_iota(jnp.int32, (1, 1, HEAD_WIDTH), 2)
    row_id = lax.broadcasted_iota(jnp.int32, (batch, 1, 1), 0)
    nt = (((1,), (1,)), ((), ()))

    def softmax_part(scores, values):
        peak = jnp.max(scores, axis=-1, keepdims=True)
        p = jnp.exp2((scores - peak) * (SCALE * LOG2E))
        total = jnp.sum(p, axis=-1, keepdims=True)
        acc = jnp.dot(p.astype(bf16), values, preferred_element_type=f32)
        return peak, total, acc

    for pair in range(PAIRS):
        if pair % (PAIRS // QUERY_CHUNKS) == 0:
            q_wait(qrecv, pair // (PAIRS // QUERY_CHUNKS))
        if pair == 0:
            for load in loads:
                load.wait()
        tile = pl.ds(pair * TILE, TILE)
        qbuf = qbufs[pair // (PAIRS // QUERY_CHUNKS)]
        q_tile = pl.ds(pair % (PAIRS // QUERY_CHUNKS) * TILE, TILE)
        slot_q = qbuf[slot_row, q_tile, :].astype(f32)
        suffix = []
        for i in range(2):
            cols = pl.ds((2 * pair + i) * HEAD_WIDTH, HEAD_WIDTH)
            q = slot_q[i * GROUP:(i + 1) * GROUP].astype(bf16)
            s = lax.dot_general(q, skbuf[:, cols], nt, preferred_element_type=f32)
            s = jnp.where(live, s, -jnp.inf)
            suffix.append(softmax_part(s, svbuf[:, cols]))

        def rows_step(b, _, pair=pair, tile=tile, suffix=suffix, qbuf=qbuf, q_tile=q_tile):
            rows = pl.ds(b * batch, batch)
            is_slot = row_id + b * batch == slot_row
            q_all = qbuf[rows, q_tile, :].astype(f32)
            outs = []
            lse_tile = lbuf[rows]
            for i in range(2):
                head = 2 * pair + i
                cols = pl.ds(head * HEAD_WIDTH, HEAD_WIDTH)
                q = q_all[:, i * GROUP:(i + 1) * GROUP, :].reshape(batch * GROUP, HEAD_WIDTH)
                s = lax.dot_general(q.astype(bf16), kbuf[:, cols], nt, preferred_element_type=f32)
                m_p, l_p, a_p = softmax_part(s, vbuf[:, cols])
                m_p = m_p.reshape(batch, GROUP, 1)
                l_p = l_p.reshape(batch, GROUP, 1)
                a_p = a_p.reshape(batch, GROUP, HEAD_WIDTH)
                m_s, l_s, a_s = suffix[i]
                m_s = jnp.where(is_slot, m_s[None], -jnp.inf)
                peak = jnp.maximum(m_p, m_s)
                f_p = jnp.exp2((m_p - peak) * (SCALE * LOG2E))
                f_s = jnp.exp2((m_s - peak) * (SCALE * LOG2E))
                total = f_p * l_p + f_s * l_s[None]
                acc = f_p * a_p + f_s * a_s[None]
                outs.append(acc / total)
                lse = peak * SCALE + jnp.log(total)
                lse_tile = jnp.where(lax.rem(lane, 8) == head, lse, lse_tile)
            obuf[rows, tile, :] = jnp.concatenate(outs, axis=1).astype(bf16)
            if pair < PAIRS - 1:
                lbuf[rows] = lse_tile
            else:
                hi = lse_tile.astype(bf16).astype(f32)
                rest = lse_tile - hi
                mid = rest.astype(bf16).astype(f32)
                parts = [jnp.where(lane < 8, hi, rest - mid), mid]
                obuf[rows, pl.ds(QUERY_HEADS, LSE_ROWS), :] = (
                    jnp.concatenate(parts, axis=1).astype(bf16))
            return 0

        if pair == 0:
            lbuf[...] = jnp.zeros_like(lbuf)
        if n == batch:
            rows_step(0, 0)
        else:
            lax.fori_loop(0, n // batch, rows_step, 0)
        if (pair + 1) % (PAIRS // OUT_CHUNKS) == 0:
            o_send(pair // (PAIRS // OUT_CHUNKS))

    rbuf[me] = obuf[me]

    fresh = fresh_ref[0].astype(f32)
    own_q = q_ref[...].astype(f32)
    new_lse = jnp.zeros((GROUP, HEAD_WIDTH), f32)
    for head in range(KEY_VALUE_HEADS):
        cols = slice(head * HEAD_WIDTH, (head + 1) * HEAD_WIDTH)
        s = jnp.sum(own_q[head * GROUP:(head + 1) * GROUP] * fresh[0:1, cols],
                    axis=-1, keepdims=True) * SCALE
        new_lse = jnp.where(lane[0] == head, s, new_lse)

    for c in range(OUT_CHUNKS):
        o_wait(orecv, c)

    parts = rbuf[:, pl.ds(QUERY_HEADS, LSE_ROWS), :].astype(f32)
    hi = parts[:, :GROUP, :]
    mid = parts[:, GROUP:, :]
    lo = pltpu.roll(hi, HEAD_WIDTH - 8, 2)
    lse = (hi + mid) + lo
    top = jnp.maximum(jnp.max(lse, axis=0), new_lse)
    weights = jnp.exp(lse - top[None])
    new_weight = jnp.exp(new_lse - top)
    inverse = 1.0 / (jnp.sum(weights, axis=0) + new_weight)
    weights = weights * inverse[None]
    new_weight = new_weight * inverse
    for pair in range(PAIRS):
        tile = pl.ds(pair * TILE, TILE)
        blocks = rbuf[:, tile, :].astype(f32)
        outs = []
        for i in range(2):
            head = 2 * pair + i
            cols = slice(head * HEAD_WIDTH, (head + 1) * HEAD_WIDTH)
            part = blocks[:, i * GROUP:(i + 1) * GROUP, :]
            acc = jnp.sum(weights[:, :, head:head + 1] * part, axis=0)
            outs.append(acc + new_weight[:, head:head + 1] * fresh[1:2, cols])
        out_ref[tile, :] = jnp.concatenate(outs, axis=0).astype(bf16)

    for c in range(QUERY_CHUNKS):
        q_wait(qsend, c)
    for c in range(OUT_CHUNKS):
        o_wait(osend, c)


def per_device(queries, prefix_key_value, suffix_key_value, fresh_key_value, lengths, home):
    n = lax.axis_size("blk")
    prefix = prefix_key_value.shape[1]
    slots = suffix_key_value.shape[2]
    width = KEY_VALUE_HEADS * HEAD_WIDTH
    q = queries.reshape(QUERY_HEADS, HEAD_WIDTH)
    bf16 = jnp.bfloat16
    flops = 4 * QUERY_HEADS * HEAD_WIDTH * (n * prefix + slots)
    out = pl.pallas_call(
        functools.partial(kernel, n),
        out_shape=jax.ShapeDtypeStruct((QUERY_HEADS, HEAD_WIDTH), bf16),
        in_specs=[
            pl.BlockSpec(memory_space=pltpu.SMEM),
            pl.BlockSpec(memory_space=pltpu.SMEM),
            pl.BlockSpec(memory_space=pltpu.VMEM),
            pl.BlockSpec(memory_space=pltpu.VMEM),
            pl.BlockSpec(memory_space=pl.ANY),
            pl.BlockSpec(memory_space=pl.ANY),
        ],
        out_specs=pl.BlockSpec(memory_space=pltpu.VMEM),
        scratch_shapes=[
            pltpu.VMEM((n, QUERY_HEADS + LSE_ROWS, HEAD_WIDTH), bf16),
            pltpu.VMEM((n, QUERY_HEADS + LSE_ROWS, HEAD_WIDTH), bf16),
            pltpu.VMEM((n, GROUP, HEAD_WIDTH), jnp.float32),
            pltpu.VMEM((prefix, width), bf16),
            pltpu.VMEM((prefix, width), bf16),
            pltpu.VMEM((slots, width), bf16),
            pltpu.VMEM((slots, width), bf16),
            pltpu.SemaphoreType.DMA((4,)),
            pltpu.SemaphoreType.DMA((QUERY_CHUNKS,)),
            pltpu.SemaphoreType.DMA((QUERY_CHUNKS,)),
            pltpu.SemaphoreType.DMA((OUT_CHUNKS,)),
            pltpu.SemaphoreType.DMA((OUT_CHUNKS,)),
        ] + [
            pltpu.VMEM((n, QUERY_HEADS // QUERY_CHUNKS, HEAD_WIDTH), bf16)
        ] * QUERY_CHUNKS,
        compiler_params=pltpu.CompilerParams(
            collective_id=0, has_side_effects=True, vmem_limit_bytes=48 * 1024 * 1024
        ),
        cost_estimate=pl.CostEstimate(
            flops=flops, bytes_accessed=4 * width * (prefix + slots),
            transcendentals=QUERY_HEADS * n * prefix,
        ),
    )(home, lengths, q, fresh_key_value, prefix_key_value, suffix_key_value)
    return out.reshape(1, QUERY_HEADS * HEAD_WIDTH)


def solution(mesh):
    placed = (
        P(("groups", "blk"), None),
        P(None, ("groups", "blk"), None),
        P(("groups", "blk"), None, None, None),
        P(("groups", "blk"), None, None),
        P("groups"),
        P("groups"),
    )
    return jax.shard_map(
        per_device,
        mesh=mesh,
        in_specs=placed,
        out_specs=P(("groups", "blk"), None),
        check_vma=False,
    )
```

time: 109 us -> 27.4 us (0.25)
  matrix products: 26.9 us -> 0 us
  blocking collectives: 24.6 us -> 0 us
  Pallas kernels: 0 us -> 22.1 us
  local copies, waits for them, and re-layouts: 22.6 us -> 4.22 us
  other arithmetic: 12.5 us -> 0.85 us
  waiting for transfers between devices: 9.97 us -> 0 us
  starting transfers between devices: 9.44 us -> 0 us
  between operations: 2.32 us -> 0.02 us
    dot_general x19 -> x0, matrix products: 26.9 us -> none  [the longest x8 14.9 us: prefix_head(): jnp.dot(exponent.astype(jnp.bfloat16), values_block, preferred_element_ty...]
    all_gather x1 -> x0, blocking collectives: 24.6 us -> none  [per_device(): gathered_parts = lax.all_gather(queries, 'blk', axis=0, tiled=True)]
    pallas_call x0 -> x1, Pallas kernels: none -> 22.1 us  [per_device(): pl.pallas_call(functools.partial(kernel, n), out_shape=jax.ShapeDtypeStru...]
    all_to_all x2 -> x0, waiting for transfers between devices: 9.97 us -> none  [the longest x1 9.97 us: per_device(): lax.all_to_all(normed_half.reshape(blocks, rows_per_block, QUERY_HEADS *...]
    all_to_all x2 -> x0, starting transfers between devices: 9.44 us -> none  [the longest x1 5.97 us: per_device(): lax.all_to_all(normed_half.reshape(blocks, rows_per_block, QUERY_HEADS *...]
    slice x2 -> x0, local copies, waits for them, and re-layouts: 5.67 us -> none  [the longest x1 3.96 us: per_device(): prefix_key_value[1]]
    unnamed x23 -> x9, local copies, waits for them, and re-layouts: 9.02 us -> 4.22 us
    another operation x7 -> x0, other arithmetic: 4.3 us -> none  [the longest x1 2.21 us: per_device(): normed_half.reshape(blocks, rows_per_block, QUERY_HEADS * HEAD_WIDTH)]
  transfers between devices with their start and end apart: 2 -> 0, of which waited for: 1 -> 0; matrix products, arithmetic and copies ran while one was open for 7% -> 0% of each run, Pallas kernels for 0% -> 0%
where the time goes in v1:
time: 27.4 us; the launch traced here: 27.2 us
  Pallas kernels  22.1 us (81%)
  local copies, waits for them, and re-layouts  4.22 us (15%)
  other arithmetic  0.85 us (3%)
    pallas_call x1, Pallas kernels, per_device(): pl.pallas_call(functools.partial(kernel, n), out_shape=jax.ShapeDtypeStru...  22.1 us
    unnamed x9, local copies, waits for them, and re-layouts  4.22 us
    unnamed x1, other arithmetic  0.85 us

profile of v1, /device:TPU:0, one launch (start us, length us, event | category | flops | bytes accessed | tf_op | source)
XLA Modules:
  0.0 27.2 jit_solution(17610545052385974414)
XLA Ops:
  0.0 0.8 %reduce = bf16[8192]{0:T(1024)(128)(2,1)S(1)} reduce(bf16[1,8192]{1,0:T(2,128)(2,1)} %param.6, bf16[]{:T(256)} %constant.3), dimensions={0}, to_apply=%param.6.reduce_sub_computation | reduce | bytes 32770 | tf_op args[0]
  0.8 0.0 copy-start
  0.9 1.6 %copy-done = bf16[1,2,512,1024]{3,2,1,0:T(8,128)(2,1)S(1)} copy-done((bf16[1,2,512,1024]{3,2,1,0:T(8,128)(2,1)S(1)}, bf16[1,2,512,1024]{3,2,1,0:T(8,128)(2,1)}, u32[]{:S(2)}) %copy-start) | copy-done | bytes 2097176
  2.4 0.0 copy-start.1
  2.4 0.7 %copy-done.1 = bf16[1,2,1024]{2,1,0:T(2,128)(2,1)S(1)} copy-done((bf16[1,2,1024]{2,1,0:T(2,128)(2,1)S(1)}, bf16[1,2,1024]{2,1,0:T(2,128)(2,1)}, u32[]{:S(2)}) %copy-start.1) | copy-done | bytes 4120
  3.1 0.0 copy-start.2
  3.1 0.7 %copy-done.2 = s32[16]{0:T(128)S(1)} copy-done((s32[16]{0:T(128)S(1)}, s32[16]{0:T(128)}, u32[]{:S(2)}) %copy-start.2) | copy-done | bytes 88
  3.8 0.0 copy-start.3
  3.8 0.7 %copy-done.3 = s32[16]{0:T(128)S(1)} copy-done((s32[16]{0:T(128)S(1)}, s32[16]{0:T(128)}, u32[]{:S(2)}) %copy-start.3) | copy-done | bytes 88
  4.4 22.1 %shard_map.64 = bf16[64,128]{1,0:T(8,128)(2,1)S(1)} custom-call(s32[16]{0:T(128)S(1)} %copy-done.2, s32[16]{0:T(128)S(1)} %copy-done.3, bf16[64,128]{1,0:T(8,128)(2,1)S(1)} %bitcast.6, bf16[1,2,1024]{2,1,0:T(2,128)(2,1)S(1)} %copy-done.1, bf16[2,1024,1024]{2,1,0:T(8,128)(2,1)} %prefix_ref.1, bf16[1,2,512,1024]{3,2,1,0:T(8,128)(2,1)S(1)} %copy-done), custom_call_target="tpu_custom_call" | custom-call | flops 553648128 | bytes 6291456 | tf_op jit(solution)/shard_map/pallas_call | solution.py:232
  26.6 0.6 %copy.9 = bf16[1,1,64,128]{3,1,2,0:T(2,128)(2,1)} copy(bf16[1,1,64,128]{3,2,1,0:T(8,128)(2,1)S(1)} %bitcast.7) | data formatting | bytes 32768
Async XLA Ops:
  0.8 1.6 %copy-start = (bf16[1,2,512,1024]{3,2,1,0:T(8,128)(2,1)S(1)}, bf16[1,2,512,1024]{3,2,1,0:T(8,128)(2,1)}, u32[]{:S(2)}) copy-start(bf16[1,2,512,1024]{3,2,1,0:T(8,128)(2,1)} %suffix_ref.1) | copy-start | bytes 6291460
  2.4 0.7 %copy-start.1 = (bf16[1,2,1024]{2,1,0:T(2,128)(2,1)S(1)}, bf16[1,2,1024]{2,1,0:T(2,128)(2,1)}, u32[]{:S(2)}) copy-start(bf16[1,2,1024]{2,1,0:T(2,128)(2,1)} %fresh_ref.1) | copy-start | bytes 12292
  3.1 0.7 %copy-start.2 = (s32[16]{0:T(128)S(1)}, s32[16]{0:T(128)}, u32[]{:S(2)}) copy-start(s32[16]{0:T(128)} %home_ref.1) | copy-start | bytes 196
  3.8 0.7 %copy-start.3 = (s32[16]{0:T(128)S(1)}, s32[16]{0:T(128)}, u32[]{:S(2)}) copy-start(s32[16]{0:T(128)} %lengths_ref.1) | copy-start | bytes 196

commit v2 on v1

v2 whole, which is shorter than its diff:
```python
import functools

import jax
import jax.numpy as jnp
from jax import lax
from jax.experimental import pallas as pl
from jax.experimental.pallas import tpu as pltpu
from jax.sharding import PartitionSpec as P

QUERY_HEADS = 64
KEY_VALUE_HEADS = 8
HEAD_WIDTH = 128
GROUP = QUERY_HEADS // KEY_VALUE_HEADS
SCALE = HEAD_WIDTH ** (-0.5)
LOG2E = 1.4426950408889634
TILE = 2 * GROUP
PAIRS = KEY_VALUE_HEADS // 2
LSE_ROWS = 16
CORES = 2
MESH = pl.DeviceIdType.MESH


def kernel(n, home_ref, lengths_ref, q_ref, fresh_ref, prefix_ref, suffix_ref, out_ref,
           home, lengths, q_in, fresh_in, xbuf, sib, obuf, rbuf, lbuf,
           kbuf, vbuf, skbuf, svbuf,
           load_sem, qsend, qrecv, fsend, frecv, ssend, srecv, osend, orecv, *qbufs):
    f32, bf16 = jnp.float32, jnp.bfloat16
    me = lax.axis_index("blk")
    chips = n // CORES
    chip, core = me // CORES, lax.rem(me, CORES)
    sibling = chip * CORES + 1 - core
    my_place = core * chips + chip
    mine = pl.ds(core * chips, chips)
    theirs = pl.ds((1 - core) * chips, chips)

    def peer_of(k):
        return lax.rem(chip + k, chips) * CORES + core

    loads = [
        pltpu.make_async_copy(q_ref, q_in, load_sem.at[0]),
        pltpu.make_async_copy(home_ref, home, load_sem.at[1]),
        pltpu.make_async_copy(lengths_ref, lengths, load_sem.at[2]),
        pltpu.make_async_copy(prefix_ref.at[0], kbuf, load_sem.at[3]),
        pltpu.make_async_copy(suffix_ref.at[0, 0], skbuf, load_sem.at[4]),
        pltpu.make_async_copy(prefix_ref.at[1], vbuf, load_sem.at[5]),
        pltpu.make_async_copy(suffix_ref.at[0, 1], svbuf, load_sem.at[6]),
        pltpu.make_async_copy(fresh_ref, fresh_in, load_sem.at[7]),
    ]
    for load in loads:
        load.start()

    barrier = pltpu.get_barrier_semaphore()
    pl.semaphore_signal(barrier, inc=1, device_id={"blk": sibling}, device_id_type=MESH)

    def greet(k, _):
        pl.semaphore_signal(barrier, inc=1, device_id={"blk": peer_of(k)}, device_id_type=MESH)
        return 0

    lax.fori_loop(1, chips, greet, 0)

    loads[0].wait()
    own_q = q_in[...].astype(f32).reshape(QUERY_HEADS, HEAD_WIDTH)
    for c in range(PAIRS):
        qbufs[c][my_place] = own_q[c * TILE:(c + 1) * TILE].astype(bf16)

    pl.semaphore_wait(barrier, chips)

    for c in range(PAIRS):
        def q_send(k, _, c=c):
            pltpu.make_async_remote_copy(
                src_ref=qbufs[c].at[my_place], dst_ref=qbufs[c].at[my_place],
                send_sem=qsend.at[c], recv_sem=qrecv.at[c],
                device_id={"blk": peer_of(k)}, device_id_type=MESH,
            ).start()
            return 0

        lax.fori_loop(1, chips, q_send, 0)

    def wait_for(part, sem):
        pltpu.make_async_copy(part, part, sem).wait()

    def forward(c):
        return pltpu.make_async_remote_copy(
            src_ref=qbufs[c].at[mine], dst_ref=qbufs[c].at[mine],
            send_sem=fsend.at[c], recv_sem=frecv.at[c],
            device_id={"blk": sibling}, device_id_type=MESH,
        )

    def swap(c):
        return pltpu.make_async_remote_copy(
            src_ref=xbuf.at[c, theirs], dst_ref=sib.at[c],
            send_sem=ssend.at[c], recv_sem=srecv.at[c],
            device_id={"blk": sibling}, device_id_type=MESH,
        )

    def o_span(c):
        return pl.ds(c * TILE, TILE + (LSE_ROWS if c == PAIRS - 1 else 0))

    def o_send(c):
        rows = o_span(c)

        def body(k, _):
            pltpu.make_async_remote_copy(
                src_ref=obuf.at[lax.rem(chip + k, chips), rows], dst_ref=rbuf.at[chip, rows],
                send_sem=osend.at[c], recv_sem=orecv.at[c],
                device_id={"blk": peer_of(k)}, device_id_type=MESH,
            ).start()
            return 0

        lax.fori_loop(1, chips, body, 0)

    loads[1].wait()
    loads[2].wait()

    def find(r, carry):
        row, length = carry
        here = home[r] == me
        return jnp.where(here, r, row), jnp.where(here, lengths[r], length)

    slot_row, slot_len = lax.fori_loop(0, n, find, (jnp.int32(0), jnp.int32(0)))
    slot_place = lax.rem(slot_row, CORES) * chips + slot_row // CORES

    batch = 16 if n % 16 == 0 else n
    live = lax.broadcasted_iota(jnp.int32, (GROUP, skbuf.shape[0]), 1) < slot_len
    lane = lax.broadcasted_iota(jnp.int32, (1, 1, HEAD_WIDTH), 2)
    row_id = lax.broadcasted_iota(jnp.int32, (batch, 1, 1), 0)
    nt = (((1,), (1,)), ((), ()))

    def softmax_part(scores, values):
        peak = jnp.max(scores, axis=-1, keepdims=True)
        p = jnp.exp2((scores - peak) * (SCALE * LOG2E))
        total = jnp.sum(p, axis=-1, keepdims=True)
        acc = jnp.dot(p.astype(bf16), values, preferred_element_type=f32)
        return peak, total, acc

    def merge(c):
        a, b = xbuf[c, mine], sib[c]
        a_lse, b_lse = a[:, TILE:], b[:, TILE:]
        top = jnp.maximum(a_lse, b_lse)
        a_w, b_w = jnp.exp(a_lse - top), jnp.exp(b_lse - top)
        total = a_w + b_w
        obuf[:, pl.ds(c * TILE, TILE), :] = (
            (a_w * a[:, :TILE] + b_w * b[:, :TILE]) / total).astype(bf16)
        lse = top + jnp.log(total)
        tile = lbuf[...]
        for i in range(2):
            tile = jnp.where(lax.rem(lane, 8) == 2 * c + i,
                             lse[:, i * GROUP:(i + 1) * GROUP], tile)
        if c < PAIRS - 1:
            lbuf[...] = tile
        else:
            hi = tile.astype(bf16).astype(f32)
            rest = tile - hi
            mid = rest.astype(bf16).astype(f32)
            parts = [jnp.where(lane < 8, hi, rest - mid), mid]
            obuf[:, pl.ds(QUERY_HEADS, LSE_ROWS), :] = (
                jnp.concatenate(parts, axis=1).astype(bf16))
        o_send(c)

    lbuf[...] = jnp.zeros_like(lbuf)

    def pass_on(c):
        wait_for(qbufs[c].at[pl.ds(0, chips - 1)], qrecv.at[c])
        forward(c).start()

    pass_on(0)
    for pair in range(PAIRS):
        if pair + 1 < PAIRS:
            pass_on(pair + 1)
        forward(pair).wait_recv()
        if pair == 0:
            for load in loads[3:]:
                load.wait()
        qbuf = qbufs[pair]
        slot_q = qbuf[slot_place].astype(f32)
        suffix = []
        for i in range(2):
            cols = pl.ds((2 * pair + i) * HEAD_WIDTH, HEAD_WIDTH)
            q = slot_q[i * GROUP:(i + 1) * GROUP].astype(bf16)
            s = lax.dot_general(q, skbuf[:, cols], nt, preferred_element_type=f32)
            s = jnp.where(live, s, -jnp.inf)
            suffix.append(softmax_part(s, svbuf[:, cols]))

        def rows_step(b, _, pair=pair, suffix=suffix, qbuf=qbuf):
            rows = pl.ds(b * batch, batch)
            is_slot = row_id + b * batch == slot_place
            q_all = qbuf[rows].astype(f32)
            outs, lses = [], []
            for i in range(2):
                cols = pl.ds((2 * pair + i) * HEAD_WIDTH, HEAD_WIDTH)
                q = q_all[:, i * GROUP:(i + 1) * GROUP, :].reshape(batch * GROUP, HEAD_WIDTH)
                s = lax.dot_general(q.astype(bf16), kbuf[:, cols], nt, preferred_element_type=f32)
                m_p, l_p, a_p = softmax_part(s, vbuf[:, cols])
                m_p = m_p.reshape(batch, GROUP, 1)
                l_p = l_p.reshape(batch, GROUP, 1)
                a_p = a_p.reshape(batch, GROUP, HEAD_WIDTH)
                m_s, l_s, a_s = suffix[i]
                m_s = jnp.where(is_slot, m_s[None], -jnp.inf)
                peak = jnp.maximum(m_p, m_s)
                f_p = jnp.exp2((m_p - peak) * (SCALE * LOG2E))
                f_s = jnp.exp2((m_s - peak) * (SCALE * LOG2E))
                total = f_p * l_p + f_s * l_s[None]
                acc = f_p * a_p + f_s * a_s[None]
                outs.append(acc / total)
                lse = peak * SCALE + jnp.log(total)
                lses.append(jnp.broadcast_to(lse, acc.shape))
            xbuf[pair, rows] = jnp.concatenate(outs + lses, axis=1)
            return 0

        if n == batch:
            rows_step(0, 0)
        else:
            lax.fori_loop(0, n // batch, rows_step, 0)
        swap(pair).start()
        if pair > 0:
            swap(pair - 1).wait_recv()
            merge(pair - 1)

    fresh = fresh_in[0].astype(f32)
    new_lse = jnp.zeros((GROUP, HEAD_WIDTH), f32)
    for head in range(KEY_VALUE_HEADS):
        cols = slice(head * HEAD_WIDTH, (head + 1) * HEAD_WIDTH)
        q = qbufs[head // 2][my_place].astype(f32)
        q = q[(head % 2) * GROUP:(head % 2 + 1) * GROUP]
        s = jnp.sum(q * fresh[0:1, cols], axis=-1, keepdims=True) * SCALE
        new_lse = jnp.where(lane[0] == head, s, new_lse)

    swap(PAIRS - 1).wait_recv()
    merge(PAIRS - 1)
    rbuf[chip] = obuf[chip]

    for c in range(PAIRS):
        wait_for(rbuf.at[pl.ds(0, chips - 1), o_span(c)], orecv.at[c])

    parts = rbuf[:, pl.ds(QUERY_HEADS, LSE_ROWS), :].astype(f32)
    hi = parts[:, :GROUP, :]
    mid = parts[:, GROUP:, :]
    lo = pltpu.roll(hi, HEAD_WIDTH - 8, 2)
    lse = (hi + mid) + lo
    top = jnp.maximum(jnp.max(lse, axis=0), new_lse)
    weights = jnp.exp(lse - top[None])
    new_weight = jnp.exp(new_lse - top)
    inverse = 1.0 / (jnp.sum(weights, axis=0) + new_weight)
    weights = weights * inverse[None]
    new_weight = new_weight * inverse
    for pair in range(PAIRS):
        tile = pl.ds(pair * TILE, TILE)
        blocks = rbuf[:, tile, :].astype(f32)
        outs = []
        for i in range(2):
            head = 2 * pair + i
            cols = slice(head * HEAD_WIDTH, (head + 1) * HEAD_WIDTH)
            part = blocks[:, i * GROUP:(i + 1) * GROUP, :]
            acc = jnp.sum(weights[:, :, head:head + 1] * part, axis=0)
            outs.append(acc + new_weight[:, head:head + 1] * fresh[1:2, cols])
        out_ref[tile, :] = jnp.concatenate(outs, axis=0).astype(bf16)

    for c in range(PAIRS):
        wait_for(qbufs[c].at[pl.ds(0, chips - 1)], qsend.at[c])
        forward(c).wait_send()
        swap(c).wait_send()
        wait_for(rbuf.at[pl.ds(0, chips - 1), o_span(c)], osend.at[c])


def per_device(queries, prefix_key_value, suffix_key_value, fresh_key_value, lengths, home):
    n = lax.axis_size("blk")
    chips = n // CORES
    prefix = prefix_key_value.shape[1]
    slots = suffix_key_value.shape[2]
    width = KEY_VALUE_HEADS * HEAD_WIDTH
    f32, bf16 = jnp.float32, jnp.bfloat16
    flops = 4 * QUERY_HEADS * HEAD_WIDTH * (n * prefix + slots)
    dma = pltpu.SemaphoreType.DMA
    out = pl.pallas_call(
        functools.partial(kernel, n),
        out_shape=jax.ShapeDtypeStruct((QUERY_HEADS, HEAD_WIDTH), bf16),
        in_specs=[pl.BlockSpec(memory_space=pl.ANY)] * 6,
        out_specs=pl.BlockSpec(memory_space=pltpu.VMEM),
        scratch_shapes=[
            pltpu.SMEM(home.shape, jnp.int32),
            pltpu.SMEM(lengths.shape, jnp.int32),
            pltpu.VMEM(queries.shape, bf16),
            pltpu.VMEM(fresh_key_value.shape, bf16),
            pltpu.VMEM((PAIRS, n, 2 * TILE, HEAD_WIDTH), f32),
            pltpu.VMEM((PAIRS, chips, 2 * TILE, HEAD_WIDTH), f32),
            pltpu.VMEM((chips, QUERY_HEADS + LSE_ROWS, HEAD_WIDTH), bf16),
            pltpu.VMEM((chips, QUERY_HEADS + LSE_ROWS, HEAD_WIDTH), bf16),
            pltpu.VMEM((chips, GROUP, HEAD_WIDTH), f32),
            pltpu.VMEM((prefix, width), bf16),
            pltpu.VMEM((prefix, width), bf16),
            pltpu.VMEM((slots, width), bf16),
            pltpu.VMEM((slots, width), bf16),
            dma((8,)),
        ] + [dma((PAIRS,))] * 8 + [
            pltpu.VMEM((n, TILE, HEAD_WIDTH), bf16)
        ] * PAIRS,
        compiler_params=pltpu.CompilerParams(
            collective_id=0, has_side_effects=True, vmem_limit_bytes=60 * 1024 * 1024
        ),
        cost_estimate=pl.CostEstimate(
            flops=flops, bytes_accessed=4 * width * (prefix + slots),
            transcendentals=QUERY_HEADS * n * prefix,
        ),
    )(home, lengths, queries, fresh_key_value, prefix_key_value, suffix_key_value)
    return out.reshape(1, QUERY_HEADS * HEAD_WIDTH)


def solution(mesh):
    placed = (
        P(("groups", "blk"), None),
        P(None, ("groups", "blk"), None),
        P(("groups", "blk"), None, None, None),
        P(("groups", "blk"), None, None),
        P("groups"),
        P("groups"),
    )
    return jax.shard_map(
        per_device,
        mesh=mesh,
        in_specs=placed,
        out_specs=P(("groups", "blk"), None),
        check_vma=False,
    )
```

time: 27.4 us -> 24.8 us (0.905)
  local copies, waits for them, and re-layouts: 4.22 us -> 1.36 us
  Pallas kernels: 22.1 us -> 23.2 us
  other arithmetic: 0.85 us -> 0 us
    unnamed x9 -> x1, local copies, waits for them, and re-layouts: 4.22 us -> 1.36 us
    pallas_call x1, Pallas kernels: 22.1 us -> 23.2 us  [per_device(): pl.pallas_call(functools.partial(kernel, n), out_shape=jax.ShapeDtypeStru...]
    unnamed x1 -> x0, other arithmetic: 0.85 us -> none
where the time goes in v2:
time: 24.8 us; the launch traced here: 24.6 us
  Pallas kernels  23.2 us (94%)
  local copies, waits for them, and re-layouts  1.36 us (5%)
    pallas_call x1, Pallas kernels, per_device(): pl.pallas_call(functools.partial(kernel, n), out_shape=jax.ShapeDtypeStru...  23.2 us
    unnamed x1, local copies, waits for them, and re-layouts  1.36 us

profile of v2, /device:TPU:0, one launch (start us, length us, event | category | flops | bytes accessed | tf_op | source)
XLA Modules:
  0.0 24.6 jit_solution(17859842682760823576)
XLA Ops:
  0.0 23.2 %shard_map.64 = bf16[64,128]{1,0:T(8,128)(2,1)} custom-call(s32[16]{0:T(128)} %home_ref.1, s32[16]{0:T(128)} %lengths_ref.1, bf16[1,8192]{1,0:T(2,128)(2,1)} %q_ref.1, bf16[1,2,1024]{2,1,0:T(2,128)(2,1)} %fresh_ref.1, bf16[2,1024,1024]{2,1,0:T(8,128)(2,1)} %prefix_ref.1, bf16[1,2,512,1024]{3,2,1,0:T(8,128)(2,1)} %suffix_ref.1), custom_call_target="tpu_custom_call" | custom-call | flops 553648128 | bytes 6291456 | tf_op jit(solution)/shard_map/pallas_call | solution.py:274
  23.2 1.4 %copy.9 = bf16[1,1,64,128]{3,1,2,0:T(2,128)(2,1)} copy(bf16[1,1,64,128]{3,2,1,0:T(8,128)(2,1)} %bitcast.5) | data formatting | bytes 32768

commit v3 on v2

--- a/solution.py
+++ b/solution.py
@@ -15,9 +15,24 @@
 LOG2E = 1.4426950408889634
 TILE = 2 * GROUP
 PAIRS = KEY_VALUE_HEADS // 2
+CHUNKS = 2
+STEP = PAIRS // CHUNKS
+ROWS = STEP * TILE
 LSE_ROWS = 16
 CORES = 2
 MESH = pl.DeviceIdType.MESH
+
+
+def each(first, last, body):
+    if last <= 8:
+        for k in range(first, last):
+            body(k)
+    else:
+        def step(k, _):
+            body(k)
+            return 0
+
+        lax.fori_loop(first, last, step, 0)
 
 
 def kernel(n, home_ref, lengths_ref, q_ref, fresh_ref, prefix_ref, suffix_ref, out_ref,
@@ -52,29 +67,27 @@
     barrier = pltpu.get_barrier_semaphore()
     pl.semaphore_signal(barrier, inc=1, device_id={"blk": sibling}, device_id_type=MESH)
 
-    def greet(k, _):
+    def greet(k):
         pl.semaphore_signal(barrier, inc=1, device_id={"blk": peer_of(k)}, device_id_type=MESH)
-        return 0
-
-    lax.fori_loop(1, chips, greet, 0)
+
+    each(1, chips, greet)
 
     loads[0].wait()
     own_q = q_in[...].astype(f32).reshape(QUERY_HEADS, HEAD_WIDTH)
-    for c in range(PAIRS):
-        qbufs[c][my_place] = own_q[c * TILE:(c + 1) * TILE].astype(bf16)
+    for c in range(CHUNKS):
+        qbufs[c][my_place] = own_q[c * ROWS:(c + 1) * ROWS].astype(bf16)
 
     pl.semaphore_wait(barrier, chips)
 
-    for c in range(PAIRS):
-        def q_send(k, _, c=c):
+    for c in range(CHUNKS):
+        def q_send(k, c=c):
             pltpu.make_async_remote_copy(
                 src_ref=qbufs[c].at[my_place], dst_ref=qbufs[c].at[my_place],
                 send_sem=qsend.at[c], recv_sem=qrecv.at[c],
                 device_id={"blk": peer_of(k)}, device_id_type=MESH,
             ).start()
-            return 0
-
-        lax.fori_loop(1, chips, q_send, 0)
+
+        each(1, chips, q_send)
 
     def wait_for(part, sem):
         pltpu.make_async_copy(part, part, sem).wait()
@@ -94,20 +107,19 @@
         )
 
     def o_span(c):
-        return pl.ds(c * TILE, TILE + (LSE_ROWS if c == PAIRS - 1 else 0))
+        return pl.ds(c * ROWS, ROWS + (LSE_ROWS if c == CHUNKS - 1 else 0))
 
     def o_send(c):
         rows = o_span(c)
 
-        def body(k, _):
+        def body(k):
             pltpu.make_async_remote_copy(
                 src_ref=obuf.at[lax.rem(chip + k, chips), rows], dst_ref=rbuf.at[chip, rows],
                 send_sem=osend.at[c], recv_sem=orecv.at[c],
                 device_id={"blk": peer_of(k)}, device_id_type=MESH,
             ).start()
-            return 0
-
-        lax.fori_loop(1, chips, body, 0)
+
+        each(1, chips, body)
 
     loads[1].wait()
     loads[2].wait()
@@ -135,18 +147,18 @@
 
     def merge(c):
         a, b = xbuf[c, mine], sib[c]
-        a_lse, b_lse = a[:, TILE:], b[:, TILE:]
+        a_lse, b_lse = a[:, ROWS:], b[:, ROWS:]
         top = jnp.maximum(a_lse, b_lse)
         a_w, b_w = jnp.exp(a_lse - top), jnp.exp(b_lse - top)
         total = a_w + b_w
-        obuf[:, pl.ds(c * TILE, TILE), :] = (
-            (a_w * a[:, :TILE] + b_w * b[:, :TILE]) / total).astype(bf16)
+        obuf[:, pl.ds(c * ROWS, ROWS), :] = (
+            (a_w * a[:, :ROWS] + b_w * b[:, :ROWS]) / total).astype(bf16)
         lse = top + jnp.log(total)
         tile = lbuf[...]
-        for i in range(2):
-            tile = jnp.where(lax.rem(lane, 8) == 2 * c + i,
+        for i in range(2 * STEP):
+            tile = jnp.where(lax.rem(lane, 8) == 2 * STEP * c + i,
                              lse[:, i * GROUP:(i + 1) * GROUP], tile)
-        if c < PAIRS - 1:
+        if c < CHUNKS - 1:
             lbuf[...] = tile
         else:
             hi = tile.astype(bf16).astype(f32)
@@ -165,14 +177,17 @@
 
     pass_on(0)
     for pair in range(PAIRS):
-        if pair + 1 < PAIRS:
-            pass_on(pair + 1)
-        forward(pair).wait_recv()
+        chunk, part = pair // STEP, pair % STEP
+        if part == 0:
+            if chunk + 1 < CHUNKS:
+                pass_on(chunk + 1)
+            forward(chunk).wait_recv()
         if pair == 0:
             for load in loads[3:]:
                 load.wait()
-        qbuf = qbufs[pair]
-        slot_q = qbuf[slot_place].astype(f32)
+        qbuf = qbufs[chunk]
+        tile = pl.ds(part * TILE, TILE)
+        slot_q = qbuf[slot_place, tile, :].astype(f32)
         suffix = []
         for i in range(2):
             cols = pl.ds((2 * pair + i) * HEAD_WIDTH, HEAD_WIDTH)
@@ -181,10 +196,10 @@
             s = jnp.where(live, s, -jnp.inf)
             suffix.append(softmax_part(s, svbuf[:, cols]))
 
-        def rows_step(b, _, pair=pair, suffix=suffix, qbuf=qbuf):
+        def rows_step(b, _, pair=pair, suffix=suffix, qbuf=qbuf, tile=tile, chunk=chunk, part=part):
             rows = pl.ds(b * batch, batch)
             is_slot = row_id + b * batch == slot_place
-            q_all = qbuf[rows].astype(f32)
+            q_all = qbuf[rows, tile, :].astype(f32)
             outs, lses = [], []
             for i in range(2):
                 cols = pl.ds((2 * pair + i) * HEAD_WIDTH, HEAD_WIDTH)
@@ -204,32 +219,33 @@
                 outs.append(acc / total)
                 lse = peak * SCALE + jnp.log(total)
                 lses.append(jnp.broadcast_to(lse, acc.shape))
-            xbuf[pair, rows] = jnp.concatenate(outs + lses, axis=1)
+            xbuf[chunk, rows, tile, :] = jnp.concatenate(outs, axis=1)
+            xbuf[chunk, rows, pl.ds(ROWS + part * TILE, TILE), :] = jnp.concatenate(lses, axis=1)
             return 0
 
         if n == batch:
             rows_step(0, 0)
         else:
             lax.fori_loop(0, n // batch, rows_step, 0)
-        swap(pair).start()
-        if pair > 0:
-            swap(pair - 1).wait_recv()
-            merge(pair - 1)
+        if part == STEP - 1:
+            swap(chunk).start()
+        if part == 0 and chunk > 0:
+            swap(chunk - 1).wait_recv()
+            merge(chunk - 1)
 
     fresh = fresh_in[0].astype(f32)
     new_lse = jnp.zeros((GROUP, HEAD_WIDTH), f32)
     for head in range(KEY_VALUE_HEADS):
         cols = slice(head * HEAD_WIDTH, (head + 1) * HEAD_WIDTH)
-        q = qbufs[head // 2][my_place].astype(f32)
-        q = q[(head % 2) * GROUP:(head % 2 + 1) * GROUP]
+        q = own_q[head * GROUP:(head + 1) * GROUP]
         s = jnp.sum(q * fresh[0:1, cols], axis=-1, keepdims=True) * SCALE
         new_lse = jnp.where(lane[0] == head, s, new_lse)
 
-    swap(PAIRS - 1).wait_recv()
-    merge(PAIRS - 1)
+    swap(CHUNKS - 1).wait_recv()
+    merge(CHUNKS - 1)
     rbuf[chip] = obuf[chip]
 
-    for c in range(PAIRS):
+    for c in range(CHUNKS):
         wait_for(rbuf.at[pl.ds(0, chips - 1), o_span(c)], orecv.at[c])
 
     parts = rbuf[:, pl.ds(QUERY_HEADS, LSE_ROWS), :].astype(f32)
@@ -243,19 +259,19 @@
     inverse = 1.0 / (jnp.sum(weights, axis=0) + new_weight)
     weights = weights * inverse[None]
     new_weight = new_weight * inverse
+    outs = []
     for pair in range(PAIRS):
         tile = pl.ds(pair * TILE, TILE)
         blocks = rbuf[:, tile, :].astype(f32)
-        outs = []
         for i in range(2):
             head = 2 * pair + i
             cols = slice(head * HEAD_WIDTH, (head + 1) * HEAD_WIDTH)
             part = blocks[:, i * GROUP:(i + 1) * GROUP, :]
             acc = jnp.sum(weights[:, :, head:head + 1] * part, axis=0)
             outs.append(acc + new_weight[:, head:head + 1] * fresh[1:2, cols])
-        out_ref[tile, :] = jnp.concatenate(outs, axis=0).astype(bf16)
-
-    for c in range(PAIRS):
+    out_ref[...] = jnp.concatenate(outs, axis=0).reshape(out_ref.shape).astype(bf16)
+
+    for c in range(CHUNKS):
         wait_for(qbufs[c].at[pl.ds(0, chips - 1)], qsend.at[c])
         forward(c).wait_send()
         swap(c).wait_send()
@@ -273,7 +289,7 @@
     dma = pltpu.SemaphoreType.DMA
     out = pl.pallas_call(
         functools.partial(kernel, n),
-        out_shape=jax.ShapeDtypeStruct((QUERY_HEADS, HEAD_WIDTH), bf16),
+        out_shape=jax.ShapeDtypeStruct(queries.shape, bf16),
         in_specs=[pl.BlockSpec(memory_space=pl.ANY)] * 6,
         out_specs=pl.BlockSpec(memory_space=pltpu.VMEM),
         scratch_shapes=[
@@ -281,8 +297,8 @@
             pltpu.SMEM(lengths.shape, jnp.int32),
             pltpu.VMEM(queries.shape, bf16),
             pltpu.VMEM(fresh_key_value.shape, bf16),
-            pltpu.VMEM((PAIRS, n, 2 * TILE, HEAD_WIDTH), f32),
-            pltpu.VMEM((PAIRS, chips, 2 * TILE, HEAD_WIDTH), f32),
+            pltpu.VMEM((CHUNKS, n, 2 * ROWS, HEAD_WIDTH), f32),
+            pltpu.VMEM((CHUNKS, chips, 2 * ROWS, HEAD_WIDTH), f32),
             pltpu.VMEM((chips, QUERY_HEADS + LSE_ROWS, HEAD_WIDTH), bf16),
             pltpu.VMEM((chips, QUERY_HEADS + LSE_ROWS, HEAD_WIDTH), bf16),
             pltpu.VMEM((chips, GROUP, HEAD_WIDTH), f32),
@@ -291,9 +307,9 @@
             pltpu.VMEM((slots, width), bf16),
             pltpu.VMEM((slots, width), bf16),
             dma((8,)),
-        ] + [dma((PAIRS,))] * 8 + [
-            pltpu.VMEM((n, TILE, HEAD_WIDTH), bf16)
-        ] * PAIRS,
+        ] + [dma((CHUNKS,))] * 8 + [
+            pltpu.VMEM((n, ROWS, HEAD_WIDTH), bf16)
+        ] * CHUNKS,
         compiler_params=pltpu.CompilerParams(
             collective_id=0, has_side_effects=True, vmem_limit_bytes=60 * 1024 * 1024
         ),
@@ -302,7 +318,7 @@
             transcendentals=QUERY_HEADS * n * prefix,
         ),
     )(home, lengths, queries, fresh_key_value, prefix_key_value, suffix_key_value)
-    return out.reshape(1, QUERY_HEADS * HEAD_WIDTH)
+    return out
 
 
 def solution(mesh):

time: 24.8 us -> 25 us (level)
  no operation moved by 1% of the time
where the time goes in v3:
time: 25 us; the launch traced here: 24.8 us
  Pallas kernels  23.4 us (94%)
  local copies, waits for them, and re-layouts  1.41 us (6%)
    pallas_call x1, Pallas kernels, per_device(): pl.pallas_call(functools.partial(kernel, n), out_shape=jax.ShapeDtypeStru...  23.4 us
    unnamed x1, local copies, waits for them, and re-layouts  1.41 us

profile of v3, /device:TPU:0, one launch (start us, length us, event | category | flops | bytes accessed | tf_op | source)
XLA Modules:
  0.0 24.8 jit_solution(8125606551308063487)
XLA Ops:
  0.0 23.4 %shard_map.64 = bf16[1,8192]{1,0:T(2,128)(2,1)} custom-call(s32[16]{0:T(128)} %home_ref.1, s32[16]{0:T(128)} %lengths_ref.1, bf16[1,8192]{1,0:T(2,128)(2,1)} %q_ref.1, bf16[1,2,1024]{2,1,0:T(2,128)(2,1)} %fresh_ref.1, bf16[2,1024,1024]{2,1,0:T(8,128)(2,1)} %prefix_ref.1, bf16[1,2,512,1024]{3,2,1,0:T(8,128)(2,1)} %suffix_ref.1), custom_call_target="tpu_custom_call" | custom-call | flops 553648128 | bytes 6291456 | tf_op jit(solution)/shard_map/pallas_call | solution.py:290
  23.4 1.4 %copy.8 = bf16[1,8192]{1,0:T(2,128)(2,1)} copy(bf16[1,8192]{1,0:T(2,128)(2,1)} %shard_map.64) | data formatting | bytes 32768

commit v4 on v3

v4 whole, which is shorter than its diff:
```python
import functools

import jax
import jax.numpy as jnp
from jax import lax
from jax.experimental import pallas as pl
from jax.experimental.pallas import tpu as pltpu
from jax.sharding import PartitionSpec as P

QUERY_HEADS = 64
KEY_VALUE_HEADS = 8
HEAD_WIDTH = 128
GROUP = QUERY_HEADS // KEY_VALUE_HEADS
SCALE = HEAD_WIDTH ** (-0.5)
LOG2E = 1.4426950408889634
TILE = 2 * GROUP
PAIRS = KEY_VALUE_HEADS // 2
BATCH = HEAD_WIDTH // GROUP
STATS = 8
CORES = 2
MESH = pl.DeviceIdType.MESH
NEW_ROWS = 16


def each(first, last, body):
    if last <= 8:
        for k in range(first, last):
            body(k)
    else:
        def step(k, _):
            body(k)
            return 0

        lax.fori_loop(first, last, step, 0)


def kernel(n, prefix, slots, home_ref, lengths_ref, q_ref, fresh_ref, prefix_ref, suffix_ref,
           out_ref, home, lengths, q_in, fresh_in, xbuf, sib, wide, obuf, rbuf, lbuf, rlse,
           kbuf, vbuf, vt,
           load_sem, qsend, qrecv, fsend, frecv, ssend, srecv, osend, orecv, lsend, lrecv,
           *qbufs):
    f32, bf16 = jnp.float32, jnp.bfloat16
    me = lax.axis_index("blk")
    chips = n // CORES
    batches = n // BATCH
    keys = prefix + slots
    chip, core = me // CORES, lax.rem(me, CORES)
    sibling = chip * CORES + 1 - core
    my_place = core * chips + chip
    mine = pl.ds(core * chips, chips)

    def peer_of(k):
        return lax.rem(chip + k, chips) * CORES + core

    loads = [
        pltpu.make_async_copy(q_ref, q_in, load_sem.at[0]),
        pltpu.make_async_copy(home_ref, home, load_sem.at[1]),
        pltpu.make_async_copy(lengths_ref, lengths, load_sem.at[2]),
        pltpu.make_async_copy(fresh_ref, fresh_in, load_sem.at[3]),
        pltpu.make_async_copy(prefix_ref.at[1], vbuf.at[pl.ds(0, prefix)], load_sem.at[4]),
        pltpu.make_async_copy(suffix_ref.at[0, 1], vbuf.at[pl.ds(prefix, slots)], load_sem.at[5]),
        pltpu.make_async_copy(prefix_ref.at[0], kbuf.at[pl.ds(0, prefix)], load_sem.at[6]),
        pltpu.make_async_copy(suffix_ref.at[0, 0], kbuf.at[pl.ds(prefix, slots)], load_sem.at[7]),
    ]
    for load in loads:
        load.start()

    barrier = pltpu.get_barrier_semaphore()
    pl.semaphore_signal(barrier, inc=1, device_id={"blk": sibling}, device_id_type=MESH)

    def greet(k):
        pl.semaphore_signal(barrier, inc=1, device_id={"blk": peer_of(k)}, device_id_type=MESH)

    each(1, chips, greet)

    loads[0].wait()
    own_q = q_in[...].astype(f32).reshape(QUERY_HEADS, HEAD_WIDTH)
    for c in range(PAIRS):
        qbufs[c][my_place] = own_q[c * TILE:(c + 1) * TILE].astype(bf16)

    pl.semaphore_wait(barrier, chips)

    for c in range(PAIRS):
        def q_send(k, c=c):
            pltpu.make_async_remote_copy(
                src_ref=qbufs[c].at[my_place], dst_ref=qbufs[c].at[my_place],
                send_sem=qsend.at[c], recv_sem=qrecv.at[c],
                device_id={"blk": peer_of(k)}, device_id_type=MESH,
            ).start()

        each(1, chips, q_send)

    def wait_for(part, sem):
        pltpu.make_async_copy(part, part, sem).wait()

    def forward(c):
        return pltpu.make_async_remote_copy(
            src_ref=qbufs[c].at[mine], dst_ref=qbufs[c].at[mine],
            send_sem=fsend.at[c], recv_sem=frecv.at[c],
            device_id={"blk": sibling}, device_id_type=MESH,
        )

    def swap(c):
        return pltpu.make_async_remote_copy(
            src_ref=xbuf.at[c], dst_ref=sib.at[c],
            send_sem=ssend.at[c], recv_sem=srecv.at[c],
            device_id={"blk": sibling}, device_id_type=MESH,
        )

    def o_send(c):
        rows = pl.ds(c * TILE, TILE)

        def body(k):
            pltpu.make_async_remote_copy(
                src_ref=obuf.at[lax.rem(chip + k, chips), rows], dst_ref=rbuf.at[chip, rows],
                send_sem=osend.at[c], recv_sem=orecv.at[c],
                device_id={"blk": peer_of(k)}, device_id_type=MESH,
            ).start()

        each(1, chips, body)

    def lse_send(k):
        place = core * chips + lax.rem(chip + k, chips)
        pltpu.make_async_remote_copy(
            src_ref=lbuf.at[place // BATCH], dst_ref=rlse.at[chip],
            send_sem=lsend, recv_sem=lrecv,
            device_id={"blk": peer_of(k)}, device_id_type=MESH,
        ).start()

    loads[1].wait()
    loads[2].wait()

    def find(r, carry):
        row, length = carry
        here = home[r] == me
        return jnp.where(here, r, row), jnp.where(here, lengths[r], length)

    slot_row, slot_len = lax.fori_loop(0, n, find, (jnp.int32(0), jnp.int32(0)))
    slot_place = lax.rem(slot_row, CORES) * chips + slot_row // CORES

    loads[3].wait()
    fresh = fresh_in[0].astype(f32)
    first = lax.broadcasted_iota(jnp.int32, (NEW_ROWS, 1), 0) == 0
    kbuf[pl.ds(keys, NEW_ROWS), :] = jnp.where(first, fresh[0:1], 0.0).astype(bf16)
    new_values = jnp.where(first, fresh[1:2], 0.0).astype(bf16)

    def turn(pair):
        for head in (2 * pair, 2 * pair + 1):
            cols = pl.ds(head * HEAD_WIDTH, HEAD_WIDTH)
            vt[cols, :] = vbuf[:, cols].T

    pair_lane = lax.broadcasted_iota(jnp.int32, (1, 2 * HEAD_WIDTH), 1)
    place_of_lane = lax.rem(pair_lane, HEAD_WIDTH) // GROUP
    slot_id = lax.broadcasted_iota(jnp.int32, (slots, 1), 0)
    stat_id = lax.broadcasted_iota(jnp.int32, (STATS, 1), 0)
    nt = (((1,), (1,)), ((), ()))
    tn = (((0,), (0,)), ((), ()))
    factor = SCALE * LOG2E

    def attend(pair, b):
        q_all = qbufs[pair][pl.ds(b * BATCH, BATCH)].astype(f32)
        q0 = q_all[:, :GROUP, :].reshape(HEAD_WIDTH, HEAD_WIDTH)
        q1 = q_all[:, GROUP:, :].reshape(HEAD_WIDTH, HEAD_WIDTH)
        zero = jnp.zeros_like(q0)
        q = jnp.concatenate([jnp.concatenate([q0, zero], axis=1),
                             jnp.concatenate([zero, q1], axis=1)], axis=0).astype(bf16)
        cols = pl.ds(pair * 2 * HEAD_WIDTH, 2 * HEAD_WIDTH)
        s = lax.dot_general(kbuf[:, cols], q, nt, preferred_element_type=f32)
        place = place_of_lane + b * BATCH
        live = slot_id < jnp.where(place == slot_place, slot_len, 0)
        s_new = jnp.where(first & (place == my_place), s[keys:], -jnp.inf)
        s = jnp.concatenate([s[:prefix], jnp.where(live, s[prefix:keys], -jnp.inf)], axis=0)
        peak = jnp.maximum(jnp.max(s, axis=0, keepdims=True),
                           jnp.max(s_new, axis=0, keepdims=True))
        p = jnp.exp2((s - peak) * factor)
        p_new = jnp.exp2((s_new - peak) * factor)
        total = jnp.sum(p, axis=0, keepdims=True) + jnp.sum(p_new, axis=0, keepdims=True)
        p, p_new = p.astype(bf16), p_new.astype(bf16)
        stats = jnp.zeros((STATS, HEAD_WIDTH), f32)
        for i in range(2):
            head = 2 * pair + i
            lanes = slice(i * HEAD_WIDTH, (i + 1) * HEAD_WIDTH)
            rows = slice(head * HEAD_WIDTH, (head + 1) * HEAD_WIDTH)
            acc = jnp.dot(vt[rows, :], p[:, lanes], preferred_element_type=f32)
            acc += lax.dot_general(new_values[:, rows], p_new[:, lanes], tn,
                                   preferred_element_type=f32)
            xbuf[pair, b, pl.ds(i * HEAD_WIDTH, HEAD_WIDTH), :] = acc
            stats = jnp.where(stat_id == i, peak[:, lanes], stats)
            stats = jnp.where(stat_id == 2 + i, total[:, lanes], stats)
        xbuf[pair, b, pl.ds(2 * HEAD_WIDTH, STATS), :] = stats

    def join(pair, b):
        x_stats = xbuf[pair, b, pl.ds(2 * HEAD_WIDTH, STATS), :]
        y_stats = sib[pair, b, pl.ds(2 * HEAD_WIDTH, STATS), :]
        outs = []
        lses = lbuf[b]
        for i in range(2):
            rows = pl.ds(i * HEAD_WIDTH, HEAD_WIDTH)
            x_m, y_m = x_stats[i:i + 1], y_stats[i:i + 1]
            peak = jnp.maximum(x_m, y_m)
            x_w, y_w = jnp.exp2((x_m - peak) * factor), jnp.exp2((y_m - peak) * factor)
            total = x_w * x_stats[2 + i:3 + i] + y_w * y_stats[2 + i:3 + i]
            inverse = 1.0 / total
            out = xbuf[pair, b, rows, :] * (x_w * inverse) + sib[pair, b, rows, :] * (y_w * inverse)
            outs.append(out.T.reshape(BATCH, GROUP, HEAD_WIDTH))
            lse = peak * SCALE + jnp.log(total)
            lses = jnp.where(stat_id == 2 * pair + i, lse, lses)
        wide[pl.ds(b * BATCH, BATCH)] = jnp.concatenate(outs, axis=1)
        lbuf[b] = lses

    def over_batches(step, pair):
        if batches == 1:
            step(pair, 0)
        else:
            def body(b, _):
                step(pair, b)
                return 0

            lax.fori_loop(0, batches, body, 0)

    def merge(pair):
        swap(pair).wait_recv()
        over_batches(join, pair)
        obuf[:, pl.ds(pair * TILE, TILE), :] = wide[mine].astype(bf16)
        o_send(pair)

    def pass_on(c):
        wait_for(qbufs[c].at[pl.ds(0, chips - 1)], qrecv.at[c])
        forward(c).start()

    lbuf[...] = jnp.zeros_like(lbuf)
    loads[4].wait()
    loads[5].wait()
    turn(0)
    pass_on(0)
    turn(1)
    loads[6].wait()
    loads[7].wait()
    for pair in range(PAIRS):
        if pair + 1 < PAIRS:
            pass_on(pair + 1)
        forward(pair).wait_recv()
        over_batches(attend, pair)
        if pair + 2 < PAIRS:
            turn(pair + 2)
        swap(pair).start()
        if pair > 0:
            merge(pair - 1)
    merge(PAIRS - 1)
    each(1, chips, lse_send)
    rbuf[chip] = obuf[chip]
    rlse[chip] = lbuf[my_place // BATCH]

    wait_for(rlse.at[pl.ds(0, chips - 1)], lrecv)
    lse = rlse[...]
    weights = jnp.exp(lse - jnp.max(lse, axis=0, keepdims=True))
    weights = weights / jnp.sum(weights, axis=0, keepdims=True)
    weights = weights.reshape(chips * KEY_VALUE_HEADS, HEAD_WIDTH)
    shift = lax.rem(HEAD_WIDTH - lax.rem(my_place, BATCH) * GROUP, HEAD_WIDTH)
    weights = pltpu.roll(weights, shift, 1).T[:GROUP]
    outs = []
    for pair in range(PAIRS):
        tile = pl.ds(pair * TILE, TILE)
        wait_for(rbuf.at[pl.ds(0, chips - 1), tile], orecv.at[pair])
        blocks = rbuf[:, tile, :].astype(f32)
        for i in range(2):
            acc = jnp.zeros((GROUP, HEAD_WIDTH), f32)
            for other in range(chips):
                at = other * KEY_VALUE_HEADS + 2 * pair + i
                acc += weights[:, at:at + 1] * blocks[other, i * GROUP:(i + 1) * GROUP, :]
            outs.append(acc)
    out_ref[...] = jnp.concatenate(outs, axis=0).reshape(out_ref.shape).astype(bf16)

    for c in range(PAIRS):
        wait_for(qbufs[c].at[pl.ds(0, chips - 1)], qsend.at[c])
        forward(c).wait_send()
        swap(c).wait_send()
        wait_for(rbuf.at[pl.ds(0, chips - 1), pl.ds(c * TILE, TILE)], osend.at[c])
    wait_for(rlse.at[pl.ds(0, chips - 1)], lsend)


def per_device(queries, prefix_key_value, suffix_key_value, fresh_key_value, lengths, home):
    n = lax.axis_size("blk")
    chips = n // CORES
    prefix = prefix_key_value.shape[1]
    slots = suffix_key_value.shape[2]
    width = KEY_VALUE_HEADS * HEAD_WIDTH
    f32, bf16 = jnp.float32, jnp.bfloat16
    flops = 4 * QUERY_HEADS * HEAD_WIDTH * (n * prefix + slots)
    dma = pltpu.SemaphoreType.DMA
    wide = 2 * HEAD_WIDTH + STATS
    batches = n // BATCH
    out = pl.pallas_call(
        functools.partial(kernel, n, prefix, slots),
        out_shape=jax.ShapeDtypeStruct(queries.shape, bf16),
        in_specs=[pl.BlockSpec(memory_space=pl.ANY)] * 6,
        out_specs=pl.BlockSpec(memory_space=pltpu.VMEM),
        scratch_shapes=[
            pltpu.SMEM(home.shape, jnp.int32),
            pltpu.SMEM(lengths.shape, jnp.int32),
            pltpu.VMEM(queries.shape, bf16),
            pltpu.VMEM(fresh_key_value.shape, bf16),
            pltpu.VMEM((PAIRS, batches, wide, HEAD_WIDTH), f32),
            pltpu.VMEM((PAIRS, batches, wide, HEAD_WIDTH), f32),
            pltpu.VMEM((n, TILE, HEAD_WIDTH), f32),
            pltpu.VMEM((chips, QUERY_HEADS, HEAD_WIDTH), bf16),
            pltpu.VMEM((chips, QUERY_HEADS, HEAD_WIDTH), bf16),
            pltpu.VMEM((batches, KEY_VALUE_HEADS, HEAD_WIDTH), f32),
            pltpu.VMEM((chips, KEY_VALUE_HEADS, HEAD_WIDTH), f32),
            pltpu.VMEM((prefix + slots + NEW_ROWS, width), bf16),
            pltpu.VMEM((prefix + slots, width), bf16),
            pltpu.VMEM((width, prefix + slots), bf16),
            dma((8,)),
        ] + [dma((PAIRS,))] * 8 + [dma, dma] + [
            pltpu.VMEM((n, TILE, HEAD_WIDTH), bf16)
        ] * PAIRS,
        compiler_params=pltpu.CompilerParams(
            collective_id=0, has_side_effects=True, vmem_limit_bytes=60 * 1024 * 1024
        ),
        cost_estimate=pl.CostEstimate(
            flops=flops, bytes_accessed=4 * width * (prefix + slots),
            transcendentals=QUERY_HEADS * n * prefix,
        ),
    )(home, lengths, queries, fresh_key_value, prefix_key_value, suffix_key_value)
    return out


def solution(mesh):
    placed = (
        P(("groups", "blk"), None),
        P(None, ("groups", "blk"), None),
        P(("groups", "blk"), None, None, None),
        P(("groups", "blk"), None, None),
        P("groups"),
        P("groups"),
    )
    return jax.shard_map(
        per_device,
        mesh=mesh,
        in_specs=placed,
        out_specs=P(("groups", "blk"), None),
        check_vma=False,
    )
```

time: 25 us -> 25.5 us (1.020)
  Pallas kernels: 23.4 us -> 24 us
    pallas_call x1, Pallas kernels: 23.4 us -> 24 us  [per_device(): pl.pallas_call(functools.partial(kernel, n, prefix, slots), out_shape=jax...]
where the time goes in v4:
time: 25.5 us; the launch traced here: 25.4 us
  Pallas kernels  24 us (94%)
  local copies, waits for them, and re-layouts  1.41 us (6%)
    pallas_call x1, Pallas kernels, per_device(): pl.pallas_call(functools.partial(kernel, n, prefix, slots), out_shape=jax...  24 us
    unnamed x1, local copies, waits for them, and re-layouts  1.41 us

profile of v4, /device:TPU:0, one launch (start us, length us, event | category | flops | bytes accessed | tf_op | source)
XLA Modules:
  0.0 25.4 jit_solution(2334475335006566722)
XLA Ops:
  0.0 24.0 %shard_map.64 = bf16[1,8192]{1,0:T(2,128)(2,1)} custom-call(s32[16]{0:T(128)} %home_ref.1, s32[16]{0:T(128)} %lengths_ref.1, bf16[1,8192]{1,0:T(2,128)(2,1)} %q_ref.1, bf16[1,2,1024]{2,1,0:T(2,128)(2,1)} %fresh_ref.1, bf16[2,1024,1024]{2,1,0:T(8,128)(2,1)} %prefix_ref.1, bf16[1,2,512,1024]{3,2,1,0:T(8,128)(2,1)} %suffix_ref.1), custom_call_target="tpu_custom_call" | custom-call | flops 553648128 | bytes 6291456 | tf_op jit(solution)/shard_map/pallas_call | solution.py:293
  24.0 1.4 %copy.8 = bf16[1,8192]{1,0:T(2,128)(2,1)} copy(bf16[1,8192]{1,0:T(2,128)(2,1)} %shard_map.64) | data formatting | bytes 32768

commit v5 on v4

--- a/solution.py
+++ b/solution.py
@@ -231,9 +231,9 @@
     lbuf[...] = jnp.zeros_like(lbuf)
     loads[4].wait()
     loads[5].wait()
-    turn(0)
+    for pair in range(PAIRS):
+        turn(pair)
     pass_on(0)
-    turn(1)
     loads[6].wait()
     loads[7].wait()
     for pair in range(PAIRS):
@@ -241,8 +241,6 @@
             pass_on(pair + 1)
         forward(pair).wait_recv()
         over_batches(attend, pair)
-        if pair + 2 < PAIRS:
-            turn(pair + 2)
         swap(pair).start()
         if pair > 0:
             merge(pair - 1)

time: 25.5 us -> 25.5 us (level)
  no operation moved by 1% of the time
where the time goes in v5:
time: 25.5 us; the launch traced here: 25.3 us
  Pallas kernels  23.9 us (94%)
  local copies, waits for them, and re-layouts  1.41 us (6%)
    pallas_call x1, Pallas kernels, per_device(): pl.pallas_call(functools.partial(kernel, n, prefix, slots), out_shape=jax...  23.9 us
    unnamed x1, local copies, waits for them, and re-layouts  1.41 us

profile of v5, /device:TPU:0, one launch (start us, length us, event | category | flops | bytes accessed | tf_op | source)
XLA Modules:
  0.0 25.3 jit_solution(7590649239241650172)
XLA Ops:
  0.0 23.9 %shard_map.64 = bf16[1,8192]{1,0:T(2,128)(2,1)} custom-call(s32[16]{0:T(128)} %home_ref.1, s32[16]{0:T(128)} %lengths_ref.1, bf16[1,8192]{1,0:T(2,128)(2,1)} %q_ref.1, bf16[1,2,1024]{2,1,0:T(2,128)(2,1)} %fresh_ref.1, bf16[2,1024,1024]{2,1,0:T(8,128)(2,1)} %prefix_ref.1, bf16[1,2,512,1024]{3,2,1,0:T(8,128)(2,1)} %suffix_ref.1), custom_call_target="tpu_custom_call" | custom-call | flops 553648128 | bytes 6291456 | tf_op jit(solution)/shard_map/pallas_call | solution.py:291
  23.9 1.4 %copy.8 = bf16[1,8192]{1,0:T(2,128)(2,1)} copy(bf16[1,8192]{1,0:T(2,128)(2,1)} %shard_map.64) | data formatting | bytes 32768

commit v6 on v5

v6 whole, which is shorter than its diff:
```python
import functools

import jax
import jax.numpy as jnp
from jax import lax
from jax.experimental import pallas as pl
from jax.experimental.pallas import tpu as pltpu
from jax.sharding import PartitionSpec as P

QUERY_HEADS = 64
KEY_VALUE_HEADS = 8
HEAD_WIDTH = 128
GROUP = QUERY_HEADS // KEY_VALUE_HEADS
SCALE = HEAD_WIDTH ** (-0.5)
LOG2E = 1.4426950408889634
TILE = 2 * GROUP
PAIRS = KEY_VALUE_HEADS // 2
BATCH = HEAD_WIDTH // GROUP
MESH = pl.DeviceIdType.MESH
NEW_ROWS = 16


def each(first, last, body):
    if last <= 16:
        for k in range(first, last):
            body(k)
    else:
        def step(k, _):
            body(k)
            return 0

        lax.fori_loop(first, last, step, 0)


def kernel(n, prefix, slots, home_ref, lengths_ref, q_ref, fresh_ref, prefix_ref, suffix_ref,
           out_ref, home, lengths, q_in, fresh_in, obuf, rbuf, lbuf, rlse,
           kbuf, vbuf, vt,
           load_sem, qsend, qrecv, osend, orecv, lsend, lrecv,
           *qbufs):
    f32, bf16 = jnp.float32, jnp.bfloat16
    me = lax.axis_index("blk")
    batches = n // BATCH
    keys = prefix + slots

    def peer_of(k):
        return k + jnp.where(k >= me, 1, 0)

    loads = [
        pltpu.make_async_copy(q_ref, q_in, load_sem.at[0]),
        pltpu.make_async_copy(home_ref, home, load_sem.at[1]),
        pltpu.make_async_copy(lengths_ref, lengths, load_sem.at[2]),
        pltpu.make_async_copy(fresh_ref, fresh_in, load_sem.at[3]),
        pltpu.make_async_copy(prefix_ref.at[1], vbuf.at[pl.ds(0, prefix)], load_sem.at[4]),
        pltpu.make_async_copy(suffix_ref.at[0, 1], vbuf.at[pl.ds(prefix, slots)], load_sem.at[5]),
        pltpu.make_async_copy(prefix_ref.at[0], kbuf.at[pl.ds(0, prefix)], load_sem.at[6]),
        pltpu.make_async_copy(suffix_ref.at[0, 0], kbuf.at[pl.ds(prefix, slots)], load_sem.at[7]),
    ]
    for load in loads:
        load.start()

    barrier = pltpu.get_barrier_semaphore()
    def greet(k):
        pl.semaphore_signal(barrier, inc=1, device_id={"blk": peer_of(k)}, device_id_type=MESH)

    each(0, n - 1, greet)

    loads[0].wait()
    own_q = q_in[...].astype(f32).reshape(QUERY_HEADS, HEAD_WIDTH)
    for c in range(PAIRS):
        qbufs[c][me] = own_q[c * TILE:(c + 1) * TILE].astype(bf16)

    pl.semaphore_wait(barrier, n - 1)

    for c in range(PAIRS):
        def q_send(k, c=c):
            k = n - 2 - k
            pltpu.make_async_remote_copy(
                src_ref=qbufs[c].at[me], dst_ref=qbufs[c].at[me],
                send_sem=qsend.at[c], recv_sem=qrecv.at[c],
                device_id={"blk": peer_of(k)}, device_id_type=MESH,
            ).start()

        each(0, n - 1, q_send)

    def wait_for(part, sem):
        pltpu.make_async_copy(part, part, sem).wait()

    def o_send(c):
        rows = pl.ds(c * TILE, TILE)

        def body(k):
            pltpu.make_async_remote_copy(
                src_ref=obuf.at[peer_of(k), rows], dst_ref=rbuf.at[me, rows],
                send_sem=osend.at[c], recv_sem=orecv.at[c],
                device_id={"blk": peer_of(k)}, device_id_type=MESH,
            ).start()

        each(0, n - 1, body)

    def lse_send(k):
        pltpu.make_async_remote_copy(
            src_ref=lbuf.at[peer_of(k) // BATCH], dst_ref=rlse.at[me],
            send_sem=lsend, recv_sem=lrecv,
            device_id={"blk": peer_of(k)}, device_id_type=MESH,
        ).start()

    loads[1].wait()
    loads[2].wait()

    def find(r, carry):
        row, length = carry
        here = home[r] == me
        return jnp.where(here, r, row), jnp.where(here, lengths[r], length)

    slot_row, slot_len = lax.fori_loop(0, n, find, (jnp.int32(0), jnp.int32(0)))

    loads[3].wait()
    fresh = fresh_in[0].astype(f32)
    first = lax.broadcasted_iota(jnp.int32, (NEW_ROWS, 1), 0) == 0
    kbuf[pl.ds(keys, NEW_ROWS), :] = jnp.where(first, fresh[0:1], 0.0).astype(bf16)
    new_values = jnp.where(first, fresh[1:2], 0.0).astype(bf16)

    def turn(pair):
        for head in (2 * pair, 2 * pair + 1):
            cols = pl.ds(head * HEAD_WIDTH, HEAD_WIDTH)
            vt[cols, :] = vbuf[:, cols].T

    pair_lane = lax.broadcasted_iota(jnp.int32, (1, 2 * HEAD_WIDTH), 1)
    place_of_lane = lax.rem(pair_lane, HEAD_WIDTH) // GROUP
    slot_id = lax.broadcasted_iota(jnp.int32, (slots, 1), 0)
    head_id = lax.broadcasted_iota(jnp.int32, (KEY_VALUE_HEADS, 1), 0)
    nt = (((1,), (1,)), ((), ()))
    tn = (((0,), (0,)), ((), ()))
    factor = SCALE * LOG2E

    def attend(pair, b):
        q_all = qbufs[pair][pl.ds(b * BATCH, BATCH)].astype(f32)
        q0 = q_all[:, :GROUP, :].reshape(HEAD_WIDTH, HEAD_WIDTH)
        q1 = q_all[:, GROUP:, :].reshape(HEAD_WIDTH, HEAD_WIDTH)
        zero = jnp.zeros_like(q0)
        q = jnp.concatenate([jnp.concatenate([q0, zero], axis=1),
                             jnp.concatenate([zero, q1], axis=1)], axis=0).astype(bf16)
        cols = pl.ds(pair * 2 * HEAD_WIDTH, 2 * HEAD_WIDTH)
        s = lax.dot_general(kbuf[:, cols], q, nt, preferred_element_type=f32)
        place = place_of_lane + b * BATCH
        live = slot_id < jnp.where(place == slot_row, slot_len, 0)
        s_new = jnp.where(first & (place == me), s[keys:], -jnp.inf)
        s = jnp.concatenate([s[:prefix], jnp.where(live, s[prefix:keys], -jnp.inf)], axis=0)
        peak = jnp.maximum(jnp.max(s, axis=0, keepdims=True),
                           jnp.max(s_new, axis=0, keepdims=True))
        p = jnp.exp2((s - peak) * factor)
        p_new = jnp.exp2((s_new - peak) * factor)
        total = jnp.sum(p, axis=0, keepdims=True) + jnp.sum(p_new, axis=0, keepdims=True)
        p, p_new = p.astype(bf16), p_new.astype(bf16)
        inverse = 1.0 / total
        lse = peak * SCALE + jnp.log(total)
        outs = []
        lses = lbuf[b]
        for i in range(2):
            head = 2 * pair + i
            lanes = slice(i * HEAD_WIDTH, (i + 1) * HEAD_WIDTH)
            rows = slice(head * HEAD_WIDTH, (head + 1) * HEAD_WIDTH)
            acc = jnp.dot(vt[rows, :], p[:, lanes], preferred_element_type=f32)
            acc += lax.dot_general(new_values[:, rows], p_new[:, lanes], tn,
                                   preferred_element_type=f32)
            out = acc * inverse[:, lanes]
            outs.append(out.T.reshape(BATCH, GROUP, HEAD_WIDTH))
            lses = jnp.where(head_id == head, lse[:, lanes], lses)
        tile = pl.ds(pair * TILE, TILE)
        obuf[pl.ds(b * BATCH, BATCH), tile, :] = jnp.concatenate(outs, axis=1).astype(bf16)
        lbuf[b] = lses

    def over_batches(step, pair):
        if batches == 1:
            step(pair, 0)
        else:
            def body(b, _):
                step(pair, b)
                return 0

            lax.fori_loop(0, batches, body, 0)

    lbuf[...] = jnp.zeros_like(lbuf)
    loads[4].wait()
    loads[5].wait()
    for pair in range(PAIRS):
        turn(pair)
    loads[6].wait()
    loads[7].wait()
    for pair in range(PAIRS):
        wait_for(qbufs[pair].at[pl.ds(0, n - 1)], qrecv.at[pair])
        over_batches(attend, pair)
        o_send(pair)
    each(0, n - 1, lse_send)
    rbuf[me] = obuf[me]
    rlse[me] = lbuf[me // BATCH]

    wait_for(rlse.at[pl.ds(0, n - 1)], lrecv)
    lse = rlse[...]
    weights = jnp.exp(lse - jnp.max(lse, axis=0, keepdims=True))
    weights = weights / jnp.sum(weights, axis=0, keepdims=True)
    weights = weights.reshape(n * KEY_VALUE_HEADS, HEAD_WIDTH)
    shift = lax.rem(HEAD_WIDTH - lax.rem(me, BATCH) * GROUP, HEAD_WIDTH)
    weights = pltpu.roll(weights, shift, 1).T[:GROUP]
    outs = []
    for pair in range(PAIRS):
        tile = pl.ds(pair * TILE, TILE)
        wait_for(rbuf.at[pl.ds(0, n - 1), tile], orecv.at[pair])
        blocks = rbuf[:, tile, :].astype(f32)
        for i in range(2):
            acc = jnp.zeros((GROUP, HEAD_WIDTH), f32)
            for other in range(n):
                at = other * KEY_VALUE_HEADS + 2 * pair + i
                acc += weights[:, at:at + 1] * blocks[other, i * GROUP:(i + 1) * GROUP, :]
            outs.append(acc)
    out_ref[...] = jnp.concatenate(outs, axis=0).reshape(out_ref.shape).astype(bf16)

    for c in range(PAIRS):
        wait_for(qbufs[c].at[pl.ds(0, n - 1)], qsend.at[c])
        wait_for(rbuf.at[pl.ds(0, n - 1), pl.ds(c * TILE, TILE)], osend.at[c])
    wait_for(rlse.at[pl.ds(0, n - 1)], lsend)


def per_device(queries, prefix_key_value, suffix_key_value, fresh_key_value, lengths, home):
    n = lax.axis_size("blk")
    prefix = prefix_key_value.shape[1]
    slots = suffix_key_value.shape[2]
    width = KEY_VALUE_HEADS * HEAD_WIDTH
    f32, bf16 = jnp.float32, jnp.bfloat16
    flops = 4 * QUERY_HEADS * HEAD_WIDTH * (n * prefix + slots)
    dma = pltpu.SemaphoreType.DMA
    batches = n // BATCH
    out = pl.pallas_call(
        functools.partial(kernel, n, prefix, slots),
        out_shape=jax.ShapeDtypeStruct(queries.shape, bf16),
        in_specs=[pl.BlockSpec(memory_space=pl.ANY)] * 6,
        out_specs=pl.BlockSpec(memory_space=pltpu.VMEM),
        scratch_shapes=[
            pltpu.SMEM(home.shape, jnp.int32),
            pltpu.SMEM(lengths.shape, jnp.int32),
            pltpu.VMEM(queries.shape, bf16),
            pltpu.VMEM(fresh_key_value.shape, bf16),
            pltpu.VMEM((n, QUERY_HEADS, HEAD_WIDTH), bf16),
            pltpu.VMEM((n, QUERY_HEADS, HEAD_WIDTH), bf16),
            pltpu.VMEM((batches, KEY_VALUE_HEADS, HEAD_WIDTH), f32),
            pltpu.VMEM((n, KEY_VALUE_HEADS, HEAD_WIDTH), f32),
            pltpu.VMEM((prefix + slots + NEW_ROWS, width), bf16),
            pltpu.VMEM((prefix + slots, width), bf16),
            pltpu.VMEM((width, prefix + slots), bf16),
            dma((8,)),
        ] + [dma((PAIRS,))] * 4 + [dma, dma] + [
            pltpu.VMEM((n, TILE, HEAD_WIDTH), bf16)
        ] * PAIRS,
        compiler_params=pltpu.CompilerParams(
            collective_id=0, has_side_effects=True, vmem_limit_bytes=60 * 1024 * 1024
        ),
        cost_estimate=pl.CostEstimate(
            flops=flops, bytes_accessed=4 * width * (prefix + slots),
            transcendentals=QUERY_HEADS * n * prefix,
        ),
    )(home, lengths, queries, fresh_key_value, prefix_key_value, suffix_key_value)
    return out


def solution(mesh):
    placed = (
        P(("groups", "blk"), None),
        P(None, ("groups", "blk"), None),
        P(("groups", "blk"), None, None, None),
        P(("groups", "blk"), None, None),
        P("groups"),
        P("groups"),
    )
    return jax.shard_map(
        per_device,
        mesh=mesh,
        in_specs=placed,
        out_specs=P(("groups", "blk"), None),
        check_vma=False,
    )
```

time: 25.5 us -> 24.4 us (0.957)
  Pallas kernels: 23.9 us -> 22.8 us
    pallas_call x1, Pallas kernels: 23.9 us -> 22.8 us  [per_device(): pl.pallas_call(functools.partial(kernel, n, prefix, slots), out_shape=jax...]
where the time goes in v6:
time: 24.4 us; the launch traced here: 24.3 us
  Pallas kernels  22.8 us (93%)
  local copies, waits for them, and re-layouts  1.41 us (6%)
    pallas_call x1, Pallas kernels, per_device(): pl.pallas_call(functools.partial(kernel, n, prefix, slots), out_shape=jax...  22.8 us
    unnamed x1, local copies, waits for them, and re-layouts  1.41 us

profile of v6, /device:TPU:0, one launch (start us, length us, event | category | flops | bytes accessed | tf_op | source)
XLA Modules:
  0.0 24.3 jit_solution(8045771788690767398)
XLA Ops:
  0.0 22.8 %shard_map.64 = bf16[1,8192]{1,0:T(2,128)(2,1)} custom-call(s32[16]{0:T(128)} %home_ref.1, s32[16]{0:T(128)} %lengths_ref.1, bf16[1,8192]{1,0:T(2,128)(2,1)} %q_ref.1, bf16[1,2,1024]{2,1,0:T(2,128)(2,1)} %fresh_ref.1, bf16[2,1024,1024]{2,1,0:T(8,128)(2,1)} %prefix_ref.1, bf16[1,2,512,1024]{3,2,1,0:T(8,128)(2,1)} %suffix_ref.1), custom_call_target="tpu_custom_call" | custom-call | flops 553648128 | bytes 6291456 | tf_op jit(solution)/shard_map/pallas_call | solution.py:233
  22.9 1.4 %copy.8 = bf16[1,8192]{1,0:T(2,128)(2,1)} copy(bf16[1,8192]{1,0:T(2,128)(2,1)} %shard_map.64) | data formatting | bytes 32768

commit v7 on v1

--- a/solution.py
+++ b/solution.py
@@ -18,60 +18,78 @@
 LSE_ROWS = 16
 QUERY_CHUNKS = 4
 OUT_CHUNKS = 4
+MESH = pl.DeviceIdType.MESH
+
+
+def each(last, body):
+    if last <= 16:
+        for k in range(last):
+            body(k)
+    else:
+        def step(k, _):
+            body(k)
+            return 0
+
+        lax.fori_loop(0, last, step, 0)
 
 
 def kernel(n, home_ref, lengths_ref, q_ref, fresh_ref, prefix_ref, suffix_ref, out_ref,
-           obuf, rbuf, lbuf, kbuf, vbuf, skbuf, svbuf,
+           home, lengths, q_in, fresh_in, obuf, rbuf, lbuf, kbuf, vbuf, skbuf, svbuf,
            load_sem, qsend, qrecv, osend, orecv, *qbufs):
     me = lax.axis_index("blk")
     f32, bf16 = jnp.float32, jnp.bfloat16
+
+    def peer_of(k):
+        return k + jnp.where(k >= me, 1, 0)
+
     loads = [
-        pltpu.make_async_copy(prefix_ref.at[0], kbuf, load_sem.at[0]),
-        pltpu.make_async_copy(prefix_ref.at[1], vbuf, load_sem.at[1]),
-        pltpu.make_async_copy(suffix_ref.at[0, 0], skbuf, load_sem.at[2]),
-        pltpu.make_async_copy(suffix_ref.at[0, 1], svbuf, load_sem.at[3]),
+        pltpu.make_async_copy(q_ref, q_in, load_sem.at[0]),
+        pltpu.make_async_copy(home_ref, home, load_sem.at[1]),
+        pltpu.make_async_copy(lengths_ref, lengths, load_sem.at[2]),
+        pltpu.make_async_copy(prefix_ref.at[0], kbuf, load_sem.at[3]),
+        pltpu.make_async_copy(suffix_ref.at[0, 0], skbuf, load_sem.at[4]),
+        pltpu.make_async_copy(prefix_ref.at[1], vbuf, load_sem.at[5]),
+        pltpu.make_async_copy(suffix_ref.at[0, 1], svbuf, load_sem.at[6]),
+        pltpu.make_async_copy(fresh_ref, fresh_in, load_sem.at[7]),
     ]
-    for load in loads:
+
+    barrier = pltpu.get_barrier_semaphore()
+
+    def greet(k):
+        pl.semaphore_signal(barrier, inc=1, device_id={"blk": peer_of(k)}, device_id_type=MESH)
+
+    loads[0].start()
+    each(n - 1, greet)
+    for load in loads[1:]:
         load.start()
 
-    barrier = pltpu.get_barrier_semaphore()
-
-    def greet(k, _):
-        peer = lax.rem(me + k, n)
-        pl.semaphore_signal(barrier, inc=1, device_id={"blk": peer},
-                            device_id_type=pl.DeviceIdType.MESH)
-        return 0
-
-    lax.fori_loop(1, n, greet, 0)
+    q_rows = QUERY_HEADS // QUERY_CHUNKS
+    loads[0].wait()
+    own_q = q_in[...].astype(f32).reshape(QUERY_HEADS, HEAD_WIDTH)
+    for c in range(QUERY_CHUNKS):
+        qbufs[c][me] = own_q[c * q_rows:(c + 1) * q_rows].astype(bf16)
+
+    pl.semaphore_wait(barrier, n - 1)
+
+    for c in range(QUERY_CHUNKS):
+        def q_send(k, c=c):
+            pltpu.make_async_remote_copy(
+                src_ref=qbufs[c].at[me], dst_ref=qbufs[c].at[me],
+                send_sem=qsend.at[c], recv_sem=qrecv.at[c],
+                device_id={"blk": peer_of(n - 2 - k)}, device_id_type=MESH,
+            ).start()
+
+        each(n - 1, q_send)
+
+    loads[1].wait()
+    loads[2].wait()
 
     def find(r, carry):
         row, length = carry
-        here = home_ref[r] == me
-        return jnp.where(here, r, row), jnp.where(here, lengths_ref[r], length)
+        here = home[r] == me
+        return jnp.where(here, r, row), jnp.where(here, lengths[r], length)
 
     slot_row, slot_len = lax.fori_loop(0, n, find, (jnp.int32(0), jnp.int32(0)))
-
-    pl.semaphore_wait(barrier, n - 1)
-
-    q_rows = QUERY_HEADS // QUERY_CHUNKS
-
-    def q_send(c):
-        rows = pl.ds(c * q_rows, q_rows)
-
-        def body(k, _):
-            peer = lax.rem(me + k, n)
-            pltpu.make_async_remote_copy(
-                src_ref=q_ref.at[rows], dst_ref=qbufs[c].at[me],
-                send_sem=qsend.at[c], recv_sem=qrecv.at[c],
-                device_id={"blk": peer}, device_id_type=pl.DeviceIdType.MESH,
-            ).start()
-            return 0
-
-        lax.fori_loop(1, n, body, 0)
-
-    for c in range(QUERY_CHUNKS):
-        q_send(c)
-        qbufs[c][me] = q_ref[pl.ds(c * q_rows, q_rows), :]
 
     def q_wait(sem, c):
         part = qbufs[c].at[pl.ds(0, n - 1)]
@@ -86,16 +104,15 @@
     def o_send(c):
         rows = o_span(c)
 
-        def body(k, _):
-            peer = lax.rem(me + k, n)
+        def body(k):
+            peer = peer_of(k)
             pltpu.make_async_remote_copy(
                 src_ref=obuf.at[peer, rows], dst_ref=rbuf.at[me, rows],
                 send_sem=osend.at[c], recv_sem=orecv.at[c],
-                device_id={"blk": peer}, device_id_type=pl.DeviceIdType.MESH,
+                device_id={"blk": peer}, device_id_type=MESH,
             ).start()
-            return 0
-
-        lax.fori_loop(1, n, body, 0)
+
+        each(n - 1, body)
 
     def o_wait(sem, c):
         part = rbuf.at[pl.ds(0, n - 1), o_span(c)]
@@ -118,7 +135,7 @@
         if pair % (PAIRS // QUERY_CHUNKS) == 0:
             q_wait(qrecv, pair // (PAIRS // QUERY_CHUNKS))
         if pair == 0:
-            for load in loads:
+            for load in loads[3:]:
                 load.wait()
         tile = pl.ds(pair * TILE, TILE)
         qbuf = qbufs[pair // (PAIRS // QUERY_CHUNKS)]
@@ -180,8 +197,7 @@
 
     rbuf[me] = obuf[me]
 
-    fresh = fresh_ref[0].astype(f32)
-    own_q = q_ref[...].astype(f32)
+    fresh = fresh_in[0].astype(f32)
     new_lse = jnp.zeros((GROUP, HEAD_WIDTH), f32)
     for head in range(KEY_VALUE_HEADS):
         cols = slice(head * HEAD_WIDTH, (head + 1) * HEAD_WIDTH)
@@ -203,17 +219,17 @@
     inverse = 1.0 / (jnp.sum(weights, axis=0) + new_weight)
     weights = weights * inverse[None]
     new_weight = new_weight * inverse
+    outs = []
     for pair in range(PAIRS):
         tile = pl.ds(pair * TILE, TILE)
         blocks = rbuf[:, tile, :].astype(f32)
-        outs = []
         for i in range(2):
             head = 2 * pair + i
             cols = slice(head * HEAD_WIDTH, (head + 1) * HEAD_WIDTH)
             part = blocks[:, i * GROUP:(i + 1) * GROUP, :]
             acc = jnp.sum(weights[:, :, head:head + 1] * part, axis=0)
             outs.append(acc + new_weight[:, head:head + 1] * fresh[1:2, cols])
-        out_ref[tile, :] = jnp.concatenate(outs, axis=0).astype(bf16)
+    out_ref[...] = jnp.concatenate(outs, axis=0).reshape(out_ref.shape).astype(bf16)
 
     for c in range(QUERY_CHUNKS):
         q_wait(qsend, c)
@@ -226,22 +242,18 @@
     prefix = prefix_key_value.shape[1]
     slots = suffix_key_value.shape[2]
     width = KEY_VALUE_HEADS * HEAD_WIDTH
-    q = queries.reshape(QUERY_HEADS, HEAD_WIDTH)
     bf16 = jnp.bfloat16
     flops = 4 * QUERY_HEADS * HEAD_WIDTH * (n * prefix + slots)
     out = pl.pallas_call(
         functools.partial(kernel, n),
-        out_shape=jax.ShapeDtypeStruct((QUERY_HEADS, HEAD_WIDTH), bf16),
-        in_specs=[
-            pl.BlockSpec(memory_space=pltpu.SMEM),
-            pl.BlockSpec(memory_space=pltpu.SMEM),
-            pl.BlockSpec(memory_space=pltpu.VMEM),
-            pl.BlockSpec(memory_space=pltpu.VMEM),
-            pl.BlockSpec(memory_space=pl.ANY),
-            pl.BlockSpec(memory_space=pl.ANY),
-        ],
+        out_shape=jax.ShapeDtypeStruct(queries.shape, bf16),
+        in_specs=[pl.BlockSpec(memory_space=pl.ANY)] * 6,
         out_specs=pl.BlockSpec(memory_space=pltpu.VMEM),
         scratch_shapes=[
+            pltpu.SMEM(home.shape, jnp.int32),
+            pltpu.SMEM(lengths.shape, jnp.int32),
+            pltpu.VMEM(queries.shape, bf16),
+            pltpu.VMEM(fresh_key_value.shape, bf16),
             pltpu.VMEM((n, QUERY_HEADS + LSE_ROWS, HEAD_WIDTH), bf16),
             pltpu.VMEM((n, QUERY_HEADS + LSE_ROWS, HEAD_WIDTH), bf16),
             pltpu.VMEM((n, GROUP, HEAD_WIDTH), jnp.float32),
@@ -249,7 +261,7 @@
             pltpu.VMEM((prefix, width), bf16),
             pltpu.VMEM((slots, width), bf16),
             pltpu.VMEM((slots, width), bf16),
-            pltpu.SemaphoreType.DMA((4,)),
+            pltpu.SemaphoreType.DMA((8,)),
             pltpu.SemaphoreType.DMA((QUERY_CHUNKS,)),
             pltpu.SemaphoreType.DMA((QUERY_CHUNKS,)),
             pltpu.SemaphoreType.DMA((OUT_CHUNKS,)),
@@ -258,14 +270,14 @@
             pltpu.VMEM((n, QUERY_HEADS // QUERY_CHUNKS, HEAD_WIDTH), bf16)
         ] * QUERY_CHUNKS,
         compiler_params=pltpu.CompilerParams(
-            collective_id=0, has_side_effects=True, vmem_limit_bytes=48 * 1024 * 1024
+            collective_id=0, has_side_effects=True, vmem_limit_bytes=60 * 1024 * 1024
         ),
         cost_estimate=pl.CostEstimate(
             flops=flops, bytes_accessed=4 * width * (prefix + slots),
             transcendentals=QUERY_HEADS * n * prefix,
         ),
-    )(home, lengths, q, fresh_key_value, prefix_key_value, suffix_key_value)
-    return out.reshape(1, QUERY_HEADS * HEAD_WIDTH)
+    )(home, lengths, queries, fresh_key_value, prefix_key_value, suffix_key_value)
+    return out
 
 
 def solution(mesh):

time: 27.4 us -> 22.9 us (0.84)
  local copies, waits for them, and re-layouts: 4.22 us -> 1.41 us
  other arithmetic: 0.85 us -> 0 us
  Pallas kernels: 22.1 us -> 21.3 us
    unnamed x9 -> x1, local copies, waits for them, and re-layouts: 4.22 us -> 1.41 us
    unnamed x1 -> x0, other arithmetic: 0.85 us -> none
    pallas_call x1, Pallas kernels: 22.1 us -> 21.3 us  [per_device(): pl.pallas_call(functools.partial(kernel, n), out_shape=jax.ShapeDtypeStru...]
where the time goes in v7:
time: 22.9 us; the launch traced here: 22.7 us
  Pallas kernels  21.3 us (93%)
  local copies, waits for them, and re-layouts  1.41 us (6%)
    pallas_call x1, Pallas kernels, per_device(): pl.pallas_call(functools.partial(kernel, n), out_shape=jax.ShapeDtypeStru...  21.3 us
    unnamed x1, local copies, waits for them, and re-layouts  1.41 us

profile of v7, /device:TPU:0, one launch (start us, length us, event | category | flops | bytes accessed | tf_op | source)
XLA Modules:
  0.0 22.7 jit_solution(16083945778171895279)
XLA Ops:
  0.0 21.3 %shard_map.64 = bf16[1,8192]{1,0:T(2,128)(2,1)} custom-call(s32[16]{0:T(128)} %home_ref.1, s32[16]{0:T(128)} %lengths_ref.1, bf16[1,8192]{1,0:T(2,128)(2,1)} %q_ref.1, bf16[1,2,1024]{2,1,0:T(2,128)(2,1)} %fresh_ref.1, bf16[2,1024,1024]{2,1,0:T(8,128)(2,1)} %prefix_ref.1, bf16[1,2,512,1024]{3,2,1,0:T(8,128)(2,1)} %suffix_ref.1), custom_call_target="tpu_custom_call" | custom-call | flops 553648128 | bytes 6291456 | tf_op jit(solution)/shard_map/pallas_call | solution.py:247
  21.3 1.4 %copy.8 = bf16[1,8192]{1,0:T(2,128)(2,1)} copy(bf16[1,8192]{1,0:T(2,128)(2,1)} %shard_map.64) | data formatting | bytes 32768

commit v8 on v7

--- a/solution.py
+++ b/solution.py
@@ -17,7 +17,8 @@
 PAIRS = KEY_VALUE_HEADS // 2
 LSE_ROWS = 16
 QUERY_CHUNKS = 4
-OUT_CHUNKS = 4
+OUT_ENDS = (2, 3, 4)
+OUT_CHUNKS = len(OUT_ENDS)
 MESH = pl.DeviceIdType.MESH
 
 
@@ -95,11 +96,10 @@
         part = qbufs[c].at[pl.ds(0, n - 1)]
         pltpu.make_async_copy(part, part, sem.at[c]).wait()
 
-    o_rows = QUERY_HEADS // OUT_CHUNKS
-
     def o_span(c):
+        start = OUT_ENDS[c - 1] * TILE if c else 0
         extra = LSE_ROWS if c == OUT_CHUNKS - 1 else 0
-        return pl.ds(c * o_rows, o_rows + extra)
+        return pl.ds(start, OUT_ENDS[c] * TILE - start + extra)
 
     def o_send(c):
         rows = o_span(c)
@@ -192,8 +192,8 @@
             rows_step(0, 0)
         else:
             lax.fori_loop(0, n // batch, rows_step, 0)
-        if (pair + 1) % (PAIRS // OUT_CHUNKS) == 0:
-            o_send(pair // (PAIRS // OUT_CHUNKS))
+        if pair + 1 in OUT_ENDS:
+            o_send(OUT_ENDS.index(pair + 1))
 
     rbuf[me] = obuf[me]
 

time: 22.9 us -> 24.3 us (1.061)
  Pallas kernels: 21.3 us -> 22.7 us
    pallas_call x1, Pallas kernels: 21.3 us -> 22.7 us  [per_device(): pl.pallas_call(functools.partial(kernel, n), out_shape=jax.ShapeDtypeStru...]
where the time goes in v8:
time: 24.3 us; the launch traced here: 24.1 us
  Pallas kernels  22.7 us (93%)
  local copies, waits for them, and re-layouts  1.41 us (6%)
    pallas_call x1, Pallas kernels, per_device(): pl.pallas_call(functools.partial(kernel, n), out_shape=jax.ShapeDtypeStru...  22.7 us
    unnamed x1, local copies, waits for them, and re-layouts  1.41 us

profile of v8, /device:TPU:0, one launch (start us, length us, event | category | flops | bytes accessed | tf_op | source)
XLA Modules:
  0.0 24.1 jit_solution(2396056025826934403)
XLA Ops:
  0.0 22.7 %shard_map.64 = bf16[1,8192]{1,0:T(2,128)(2,1)} custom-call(s32[16]{0:T(128)} %home_ref.1, s32[16]{0:T(128)} %lengths_ref.1, bf16[1,8192]{1,0:T(2,128)(2,1)} %q_ref.1, bf16[1,2,1024]{2,1,0:T(2,128)(2,1)} %fresh_ref.1, bf16[2,1024,1024]{2,1,0:T(8,128)(2,1)} %prefix_ref.1, bf16[1,2,512,1024]{3,2,1,0:T(8,128)(2,1)} %suffix_ref.1), custom_call_target="tpu_custom_call" | custom-call | flops 553648128 | bytes 6291456 | tf_op jit(solution)/shard_map/pallas_call | solution.py:247
  22.7 1.4 %copy.8 = bf16[1,8192]{1,0:T(2,128)(2,1)} copy(bf16[1,8192]{1,0:T(2,128)(2,1)} %shard_map.64) | data formatting | bytes 32768

commit v9 on v7

--- a/solution.py
+++ b/solution.py
@@ -18,6 +18,8 @@
 LSE_ROWS = 16
 QUERY_CHUNKS = 4
 OUT_CHUNKS = 4
+CORES = 2
+DIRECT = 2
 MESH = pl.DeviceIdType.MESH
 
 
@@ -35,12 +37,29 @@
 
 def kernel(n, home_ref, lengths_ref, q_ref, fresh_ref, prefix_ref, suffix_ref, out_ref,
            home, lengths, q_in, fresh_in, obuf, rbuf, lbuf, kbuf, vbuf, skbuf, svbuf,
-           load_sem, qsend, qrecv, osend, orecv, *qbufs):
+           load_sem, qsend, qrecv, fsend, frecv, osend, orecv, *qbufs):
     me = lax.axis_index("blk")
     f32, bf16 = jnp.float32, jnp.bfloat16
 
     def peer_of(k):
         return k + jnp.where(k >= me, 1, 0)
+
+    chips = n // CORES
+    chip, core = me // CORES, lax.rem(me, CORES)
+    sibling = chip * CORES + 1 - core
+
+    def place_of(block):
+        return lax.rem(block, CORES) * chips + block // CORES
+
+    my_place = place_of(me)
+    mine = pl.ds(core * chips, chips)
+
+    def forward(c):
+        return pltpu.make_async_remote_copy(
+            src_ref=qbufs[c].at[mine], dst_ref=qbufs[c].at[mine],
+            send_sem=fsend.at[c], recv_sem=frecv.at[c],
+            device_id={"blk": sibling}, device_id_type=MESH,
+        )
 
     loads = [
         pltpu.make_async_copy(q_ref, q_in, load_sem.at[0]),
@@ -67,19 +86,24 @@
     loads[0].wait()
     own_q = q_in[...].astype(f32).reshape(QUERY_HEADS, HEAD_WIDTH)
     for c in range(QUERY_CHUNKS):
-        qbufs[c][me] = own_q[c * q_rows:(c + 1) * q_rows].astype(bf16)
+        qbufs[c][my_place] = own_q[c * q_rows:(c + 1) * q_rows].astype(bf16)
 
     pl.semaphore_wait(barrier, n - 1)
 
     for c in range(QUERY_CHUNKS):
         def q_send(k, c=c):
+            if c < DIRECT:
+                peer = peer_of(n - 2 - k)
+            else:
+                other = chips - 2 - k
+                peer = (other + jnp.where(other >= chip, 1, 0)) * CORES + core
             pltpu.make_async_remote_copy(
-                src_ref=qbufs[c].at[me], dst_ref=qbufs[c].at[me],
+                src_ref=qbufs[c].at[my_place], dst_ref=qbufs[c].at[my_place],
                 send_sem=qsend.at[c], recv_sem=qrecv.at[c],
-                device_id={"blk": peer_of(n - 2 - k)}, device_id_type=MESH,
+                device_id={"blk": peer}, device_id_type=MESH,
             ).start()
 
-        each(n - 1, q_send)
+        each(n - 1 if c < DIRECT else chips - 1, q_send)
 
     loads[1].wait()
     loads[2].wait()
@@ -89,10 +113,11 @@
         here = home[r] == me
         return jnp.where(here, r, row), jnp.where(here, lengths[r], length)
 
-    slot_row, slot_len = lax.fori_loop(0, n, find, (jnp.int32(0), jnp.int32(0)))
+    slot_block, slot_len = lax.fori_loop(0, n, find, (jnp.int32(0), jnp.int32(0)))
+    slot_row = place_of(slot_block)
 
     def q_wait(sem, c):
-        part = qbufs[c].at[pl.ds(0, n - 1)]
+        part = qbufs[c].at[pl.ds(0, n - 1 if c < DIRECT else chips - 1)]
         pltpu.make_async_copy(part, part, sem.at[c]).wait()
 
     o_rows = QUERY_HEADS // OUT_CHUNKS
@@ -107,7 +132,7 @@
         def body(k):
             peer = peer_of(k)
             pltpu.make_async_remote_copy(
-                src_ref=obuf.at[peer, rows], dst_ref=rbuf.at[me, rows],
+                src_ref=obuf.at[place_of(peer), rows], dst_ref=rbuf.at[me, rows],
                 send_sem=osend.at[c], recv_sem=orecv.at[c],
                 device_id={"blk": peer}, device_id_type=MESH,
             ).start()
@@ -133,7 +158,14 @@
 
     for pair in range(PAIRS):
         if pair % (PAIRS // QUERY_CHUNKS) == 0:
-            q_wait(qrecv, pair // (PAIRS // QUERY_CHUNKS))
+            c = pair // (PAIRS // QUERY_CHUNKS)
+            if c < DIRECT:
+                q_wait(qrecv, c)
+            else:
+                forward(c).wait_recv()
+            if c > 0 and DIRECT <= c + 1 < QUERY_CHUNKS:
+                q_wait(qrecv, c + 1)
+                forward(c + 1).start()
         if pair == 0:
             for load in loads[3:]:
                 load.wait()
@@ -195,7 +227,7 @@
         if (pair + 1) % (PAIRS // OUT_CHUNKS) == 0:
             o_send(pair // (PAIRS // OUT_CHUNKS))
 
-    rbuf[me] = obuf[me]
+    rbuf[me] = obuf[my_place]
 
     fresh = fresh_in[0].astype(f32)
     new_lse = jnp.zeros((GROUP, HEAD_WIDTH), f32)
@@ -233,6 +265,8 @@
 
     for c in range(QUERY_CHUNKS):
         q_wait(qsend, c)
+        if c >= DIRECT:
+            forward(c).wait_send()
     for c in range(OUT_CHUNKS):
         o_wait(osend, c)
 
@@ -264,6 +298,8 @@
             pltpu.SemaphoreType.DMA((8,)),
             pltpu.SemaphoreType.DMA((QUERY_CHUNKS,)),
             pltpu.SemaphoreType.DMA((QUERY_CHUNKS,)),
+            pltpu.SemaphoreType.DMA((QUERY_CHUNKS,)),
+            pltpu.SemaphoreType.DMA((QUERY_CHUNKS,)),
             pltpu.SemaphoreType.DMA((OUT_CHUNKS,)),
             pltpu.SemaphoreType.DMA((OUT_CHUNKS,)),
         ] + [

time: 22.9 us -> 23.3 us (1.017)
  Pallas kernels: 21.3 us -> 21.7 us
    pallas_call x1, Pallas kernels: 21.3 us -> 21.7 us  [per_device(): pl.pallas_call(functools.partial(kernel, n), out_shape=jax.ShapeDtypeStru...]
where the time goes in v9:
time: 23.3 us; the launch traced here: 23.2 us
  Pallas kernels  21.7 us (93%)
  local copies, waits for them, and re-layouts  1.41 us (6%)
    pallas_call x1, Pallas kernels, per_device(): pl.pallas_call(functools.partial(kernel, n), out_shape=jax.ShapeDtypeStru...  21.7 us
    unnamed x1, local copies, waits for them, and re-layouts  1.41 us

profile of v9, /device:TPU:0, one launch (start us, length us, event | category | flops | bytes accessed | tf_op | source)
XLA Modules:
  0.0 23.2 jit_solution(13637601216622075114)
XLA Ops:
  0.0 21.7 %shard_map.64 = bf16[1,8192]{1,0:T(2,128)(2,1)} custom-call(s32[16]{0:T(128)} %home_ref.1, s32[16]{0:T(128)} %lengths_ref.1, bf16[1,8192]{1,0:T(2,128)(2,1)} %q_ref.1, bf16[1,2,1024]{2,1,0:T(2,128)(2,1)} %fresh_ref.1, bf16[2,1024,1024]{2,1,0:T(8,128)(2,1)} %prefix_ref.1, bf16[1,2,512,1024]{3,2,1,0:T(8,128)(2,1)} %suffix_ref.1), custom_call_target="tpu_custom_call" | custom-call | flops 553648128 | bytes 6291456 | tf_op jit(solution)/shard_map/pallas_call | solution.py:281
  21.8 1.4 %copy.8 = bf16[1,8192]{1,0:T(2,128)(2,1)} copy(bf16[1,8192]{1,0:T(2,128)(2,1)} %shard_map.64) | data formatting | bytes 32768

commit v10 on v7

--- a/solution.py
+++ b/solution.py
@@ -170,8 +170,8 @@
                 f_p = jnp.exp2((m_p - peak) * (SCALE * LOG2E))
                 f_s = jnp.exp2((m_s - peak) * (SCALE * LOG2E))
                 total = f_p * l_p + f_s * l_s[None]
-                acc = f_p * a_p + f_s * a_s[None]
-                outs.append(acc / total)
+                inverse = 1.0 / total
+                outs.append((f_p * inverse) * a_p + (f_s * inverse) * a_s[None])
                 lse = peak * SCALE + jnp.log(total)
                 lse_tile = jnp.where(lax.rem(lane, 8) == head, lse, lse_tile)
             obuf[rows, tile, :] = jnp.concatenate(outs, axis=1).astype(bf16)

time: 22.9 us -> 22.9 us (level)
  no operation moved by 1% of the time
where the time goes in v10:
time: 22.9 us; the launch traced here: 22.7 us
  Pallas kernels  21.3 us (93%)
  local copies, waits for them, and re-layouts  1.41 us (6%)
    pallas_call x1, Pallas kernels, per_device(): pl.pallas_call(functools.partial(kernel, n), out_shape=jax.ShapeDtypeStru...  21.3 us
    unnamed x1, local copies, waits for them, and re-layouts  1.41 us

profile of v10, /device:TPU:0, one launch (start us, length us, event | category | flops | bytes accessed | tf_op | source)
XLA Modules:
  0.0 22.7 jit_solution(1101806162201472874)
XLA Ops:
  0.0 21.3 %shard_map.64 = bf16[1,8192]{1,0:T(2,128)(2,1)} custom-call(s32[16]{0:T(128)} %home_ref.1, s32[16]{0:T(128)} %lengths_ref.1, bf16[1,8192]{1,0:T(2,128)(2,1)} %q_ref.1, bf16[1,2,1024]{2,1,0:T(2,128)(2,1)} %fresh_ref.1, bf16[2,1024,1024]{2,1,0:T(8,128)(2,1)} %prefix_ref.1, bf16[1,2,512,1024]{3,2,1,0:T(8,128)(2,1)} %suffix_ref.1), custom_call_target="tpu_custom_call" | custom-call | flops 553648128 | bytes 6291456 | tf_op jit(solution)/shard_map/pallas_call | solution.py:247
  21.3 1.4 %copy.8 = bf16[1,8192]{1,0:T(2,128)(2,1)} copy(bf16[1,8192]{1,0:T(2,128)(2,1)} %shard_map.64) | data formatting | bytes 32768
